TPU v7x, 512 devices: a whole 4x4x16 slice. The times are simulated.
512 devices in a mesh: section: 2 (over core), tile: 128 (over z_lo, y, x), sub: 2 (over z_hi).
Axes of the slice: x: 4, y: 4, z: 16 (z_hi: 2, z_lo: 8; z = z_hi * 8 + z_lo), core: 2. Of those that a mesh axis runs over, the one named last changes fastest.
Arguments:
- traces: float32 [16384, 8, 1024], P(('section', 'tile', 'sub')), may hold values from -6 to 6
- band_gain: float32 [1024], replicated, may hold values from 0.2 to 2
- aperture: int32 [16384, 4], P(('section', 'tile', 'sub')), may hold values from 0 to 127, all different within a row; in each aligned block of 32 rows (0 to 31, 32 to 63, ...) at most 2 rows name the same one
- taper: float32 [16384, 4], P(('section', 'tile', 'sub')), may hold values from 0.25 to 1
- weights: float32 [128, 1024, 1536], P('tile', None, ('section', 'sub')), may hold values from -0.375 to 0.375
- spread: float32 [128, 8, 128], P('tile'), may hold values from -3 to 3
Outputs:
- image: float32 [128, 1536, 128], P('tile', ('section', 'sub'))
Inputs may be any that keep to these rules, and one draw needn't show every extreme that they name: `aperture`: each row names 4 different tiles; among the 32 rows of one device no tile is named more than 2 times, a bound that some block reaches; every tile is named by some row.
All inputs are finite; a program needn't handle non-finite values.
Results may differ from a plain program's by a relative error of at most 0.000094.
Values sent between devices are 32-bit elements; how exact they have to be, the bound alone decides.
No kernel may reach another device: no remote copies, remote signals or barrier semaphores. Data moves between devices by JAX's collectives and lax.ppermute only.
A program may use at most 64 MiB of HBM per device.

v0:
```python
import math

import jax
import jax.numpy as jnp
from jax import lax
from jax.sharding import PartitionSpec as P


def fourier_table(samples):
    sample_index = jnp.arange(samples, dtype=jnp.int32)
    phase_index = sample_index[:, None] * sample_index[None, :] % samples
    angles = phase_index.astype(jnp.float32) * (2.0 * math.pi / samples)
    return jnp.concatenate([jnp.cos(angles), jnp.sin(angles)], axis=1)


def body(traces, band_gain, aperture, taper, weights, spread):
    tile_count = lax.axis_size("tile")
    blocks, per_block, samples = traces.shape
    list_width = aperture.shape[1]
    table_both = fourier_table(samples)
    trace_rows = traces.reshape(blocks * per_block, samples)
    spectra = jnp.dot(
        trace_rows, table_both, precision=lax.Precision.HIGHEST, preferred_element_type=jnp.float32
    )
    spectra = spectra * jnp.concatenate([band_gain, band_gain])[None, :]
    filtered = (
        lax.dot_general(
            spectra,
            table_both,
            (((1,), (1,)), ((), ())),
            precision=lax.Precision.HIGHEST,
            preferred_element_type=jnp.float32,
        )
        / samples
    )
    flat_blocks = filtered.reshape(blocks, per_block * samples)
    tile_ids = jnp.arange(tile_count, dtype=jnp.int32)
    one_hot = (aperture[:, :, None] == tile_ids[None, None, :]).astype(jnp.float32)
    capacity = max(2, min(blocks, 2 * blocks * list_width // tile_count))
    entry_total = blocks * list_width
    entries = one_hot.reshape(entry_total, tile_count)
    entry_index = jnp.arange(entry_total, dtype=jnp.int32)
    earlier_mask = (entry_index[:, None] > entry_index[None, :]).astype(jnp.float32)
    earlier = jnp.dot(earlier_mask, entries, preferred_element_type=jnp.float32)
    slot_index = jnp.sum(earlier * entries, axis=1)
    slot_hot = (slot_index[:, None] == jnp.arange(capacity, dtype=jnp.float32)[None, :]).astype(
        jnp.float32
    )
    chooser = entries[:, :, None] * slot_hot[:, None, :]
    filled = jnp.sum(chooser, axis=0)
    weighted = chooser * taper.reshape(entry_total)[:, None, None]
    block_pick = jnp.sum(weighted.reshape(blocks, list_width, tile_count * capacity), axis=1)
    packed = lax.dot_general(
        block_pick,
        flat_blocks,
        (((0,), (0,)), ((), ())),
        precision=lax.Precision.HIGHEST,
        preferred_element_type=jnp.float32,
    )
    packed = packed.reshape(tile_count, capacity, per_block * samples)
    received, filled_in = (
        lax.all_to_all(packed, "tile", split_axis=0, concat_axis=0, tiled=True),
        lax.all_to_all(filled, "tile", split_axis=0, concat_axis=0, tiled=True),
    )
    local_sum = jnp.sum(received, axis=(0, 1))
    fold_local = jnp.sum(filled_in)
    stacked_sum, fold_count = lax.psum((local_sum, fold_local), ("section", "sub"))
    stacked = stacked_sum.reshape(per_block, samples)
    focused = jnp.dot(
        stacked, weights[0], precision=lax.Precision.HIGHEST, preferred_element_type=jnp.float32
    )
    image_slab = lax.dot_general(
        focused,
        spread[0],
        (((0,), (0,)), ((), ())),
        precision=lax.Precision.HIGHEST,
        preferred_element_type=jnp.float32,
    )
    return (image_slab / jnp.sqrt(fold_count))[None]


def solution(mesh):
    placed = (
        P(("section", "tile", "sub"), None, None),
        P(),
        P(("section", "tile", "sub"), None),
        P(("section", "tile", "sub"), None),
        P("tile", None, ("section", "sub")),
        P("tile", None, None),
    )
    return jax.shard_map(
        body,
        mesh=mesh,
        in_specs=placed,
        out_specs=P("tile", ("section", "sub"), None),
        check_vma=False,
    )
```

profile of v0, /device:TPU:1, one launch (start us, length us, event | category | flops | bytes accessed | tf_op | source)
XLA Modules:
  0.0 524.8 jit_solution(14826815424674677021)
XLA Ops:
  0.0 0.0 copy-start
  0.0 0.9 copy.13
  0.9 0.1 eq.40
  1.0 0.2 fusion.15
  1.2 0.8 fusion.24
  2.1 20.4 %all-to-all-start.1 = ((f32[128,1,2]{2,1,0:T(1,128)}), f32[128,1,2]{2,1,0:T(1,128)S(1)}, u32[]{:S(2)}, u32[]{:S(2)}) async-start(f32[128,1,2]{2,1,0:T(1,128)} %bitcast.5), calls=%async_computation.1 | async-start | bytes 131072 | tf_op jit(solution)/shard_map/all_to_all | solution.py:63
  22.5 0.0 copy-start.4
  22.5 0.0 copy-start.5
  22.5 17.6 %fusion.9 = (f32[1024,1024]{1,0:T(8,128)}, f32[1024,1024]{1,0:T(8,128)}) fusion(), kind=kLoop, calls=%fused_computation.14 | loop fusion | flops 14680064 | bytes 8388608 | tf_op jit(solution)/shard_map/sin | solution.py:13
  40.0 0.0 copy-done.4
  40.1 0.0 copy-start.3
  40.1 0.0 copy-done.5
  40.1 0.1 copy.14
  40.2 5.6 %mul.69 = f32[32,4,256]{1,0,2:T(8,128)} reshape(f32[128,128,2]{0,2,1:T(2,128)S(1)} %get-tuple-element.8) | data formatting | bytes 262144 | tf_op jit(solution)/shard_map/mul | solution.py:49
  45.8 0.0 copy-done.3
  45.8 16.4 %fusion.8 = f32[2048,256]{1,0:T(8,128)S(1)} fusion(f32[1024,1024]{1,0:T(8,128)} %get-tuple-element.9, f32[1024,1024]{1,0:T(8,128)} %get-tuple-element.10, f32[32,8,1024]{2,1,0:T(8,128)S(1)} %copy-done.3, f32[2048]{0:T(1024)S(1)} %pad_maximum_fusion.7), kind=kOutput, calls=%fused_computation.13 | convolution fusion | flops 6445072384 | bytes 11542528 | tf_op jit(solution)/shard_map/dot_general | solution.py:22
  62.2 0.0 copy-done.1
  62.2 0.0 copy-done.2
  62.3 15.1 %fusion.13 = f32[256,1024]{1,0:T(8,128)} fusion(f32[2048,256]{1,0:T(8,128)S(1)} %fusion.8, f32[1024,1024]{1,0:T(8,128)S(1)} %copy-done.1, f32[1024,1024]{1,0:T(8,128)S(1)} %copy-done.2), kind=kOutput, calls=%fused_computation.18 | convolution fusion | flops 6444810240 | bytes 11534336 | tf_op jit(solution)/shard_map/dot_general | solution.py:27
  77.4 1.4 reshape.63
  78.8 3.3 multiply_reduce_fusion
  82.1 6.7 %fusion.17 = f32[128,2,8192]{2,0,1:T(8,128)S(1)} fusion(f32[32,8192,1]{1,0,2:T(8,128)S(1)} %reshape.63, f32[128,2,32]{2,1,0:T(2,128)S(1)} %bitcast.21), kind=kOutput, calls=%fused_computation.24 | convolution fusion | flops 805306368 | bytes 9469952 | tf_op jit(solution)/shard_map/dot_general | solution.py:53
  88.9 8.2 %copy.16 = f32[128,2,8192]{2,1,0:T(2,128)} copy(f32[128,2,8192]{2,0,1:T(8,128)S(1)} %fusion.17) | data formatting | bytes 16777216 | tf_op jit(solution)/shard_map/dot_general | solution.py:53
  97.0 0.0 all-to-all-done.1
  97.0 17.0 %all-to-all-start = ((f32[128,2,8192]{2,1,0:T(2,128)}), f32[128,2,8192]{2,1,0:T(2,128)}, u32[]{:S(2)}, u32[]{:S(2)}) async-start(f32[128,2,8192]{2,1,0:T(2,128)} %copy.16), calls=%async_computation | async-start | bytes 16777216 | tf_op jit(solution)/shard_map/all_to_all | solution.py:62
  114.0 0.7 reduce_sum.49
  114.7 362.7 %all-to-all-done = f32[128,2,8192]{2,1,0:T(2,128)} async-done(((f32[128,2,8192]{2,1,0:T(2,128)}), f32[128,2,8192]{2,1,0:T(2,128)}, u32[]{:S(2)}, u32[]{:S(2)}) %all-to-all-start) | async-done | bytes 8388640 | tf_op jit(solution)/shard_map/all_to_all | solution.py:62
  477.5 5.8 %reduce_sum.47 = f32[8192]{0:T(1024)S(1)} reduce(f32[128,2,8192]{2,1,0:T(2,128)} %all-to-all-done, f32[]{:T(128)} %constant.17.clone.1), dimensions={0,1}, to_apply=%region_2.3 | reduce | flops 2088960 | bytes 8421380 | tf_op jit(solution)/shard_map/reduce_sum | solution.py:65
  483.3 38.5 %all-reduce = (f32[8,1024]{1,0:T(8,128)S(1)}, f32[]{:T(128)}) all-reduce(f32[8,1024]{1,0:T(8,128)S(1)} %reshape.62, f32[]{:T(128)} %reduce_sum.49), channel_id=1, replica_groups=mesh['section'=2,'tile'=128,'sub'=2] {'section','sub'}, use_global_device_ids=true, to_apply=%region_3.4 | all-reduce | flops 8193 | bytes 65544 | tf_op jit(solution)/shard_map/psum | solution.py:67
  522.5 0.8 fusion.11
  523.3 0.0 copy-done.6
  523.3 1.2 fusion.14
  (8 shorter events, 0.0 us)
Async XLA Ops:
  0.0 522.5 %copy-start = (f32[1,1024,384]{2,1,0:T(8,128)S(1)}, f32[1,1024,384]{2,1,0:T(8,128)}, u32[]{:S(2)}) copy-start(f32[1,1024,384]{2,1,0:T(8,128)} %param.10) | copy-start | bytes 4718596
  2.1 95.0 %all-to-all-start.1 = ((f32[128,1,2]{2,1,0:T(1,128)}), f32[128,1,2]{2,1,0:T(1,128)S(1)}, u32[]{:S(2)}, u32[]{:S(2)}) async-start(f32[128,1,2]{2,1,0:T(1,128)} %bitcast.5), calls=%async_computation.1 | async-start | bytes 131072 | tf_op jit(solution)/shard_map/all_to_all | solution.py:63
  22.5 17.6 %copy-start.4 = (f32[1024]{0:T(1024)S(1)}, f32[1024]{0:T(1024)}, u32[]{:S(2)}) copy-start(f32[1024]{0:T(1024)} %param.7) | copy-start | bytes 12292
  22.5 17.6 %copy-start.5 = (f32[32,4]{0,1:T(4,128)S(1)}, f32[32,4]{0,1:T(4,128)}, u32[]{:S(2)}) copy-start(f32[32,4]{0,1:T(4,128)} %param.9) | copy-start | bytes 1540
  40.1 5.7 %copy-start.3 = (f32[32,8,1024]{2,1,0:T(8,128)S(1)}, f32[32,8,1024]{2,1,0:T(8,128)}, u32[]{:S(2)}) copy-start(f32[32,8,1024]{2,1,0:T(8,128)} %param.6) | copy-start | bytes 3145732
  45.8 16.4 %copy-start.1 = (f32[1024,1024]{1,0:T(8,128)S(1)}, f32[1024,1024]{1,0:T(8,128)}, u32[]{:S(2)}) copy-start(f32[1024,1024]{1,0:T(8,128)} %get-tuple-element.9) | copy-start | bytes 12582916
  45.8 16.5 %copy-start.2 = (f32[1024,1024]{1,0:T(8,128)S(1)}, f32[1024,1024]{1,0:T(8,128)}, u32[]{:S(2)}) copy-start(f32[1024,1024]{1,0:T(8,128)} %get-tuple-element.10) | copy-start | bytes 12582916
  97.0 380.4 %all-to-all-start = ((f32[128,2,8192]{2,1,0:T(2,128)}), f32[128,2,8192]{2,1,0:T(2,128)}, u32[]{:S(2)}, u32[]{:S(2)}) async-start(f32[128,2,8192]{2,1,0:T(2,128)} %copy.16), calls=%async_computation | async-start | bytes 16777216 | tf_op jit(solution)/shard_map/all_to_all | solution.py:62
  114.7 408.6 %copy-start.6 = (f32[1,8,128]{2,1,0:T(8,128)S(1)}, f32[1,8,128]{2,1,0:T(8,128)}, u32[]{:S(2)}) copy-start(f32[1,8,128]{2,1,0:T(8,128)} %param.11) | copy-start | bytes 12292
where the time goes:
time: 533 us; the launch traced here: 525 us
  waiting for transfers between devices  363 us (68%)
  matrix products  40.4 us (8%)
  blocking collectives  38.5 us (7%)
  starting transfers between devices  37.4 us (7%)
  other arithmetic  28.3 us (5%)
  local copies, waits for them, and re-layouts  16.3 us (3%)
    all_to_all x1, waiting for transfers between devices, body(): lax.all_to_all(packed, 'tile', split_axis=0, concat_axis=0, tiled=True)  363 us
    psum x1, blocking collectives, body(): lax.psum((local_sum, fold_local), ('section', 'sub'))  38.5 us
    all_to_all x1, starting transfers between devices, body(): lax.all_to_all(filled, 'tile', split_axis=0, concat_axis=0, tiled=True)  20.4 us
    sin x1, other arithmetic, fourier_table(): return jnp.concatenate([jnp.cos(angles), jnp.sin(angles)], axis=1)  17.6 us
    all_to_all x1, starting transfers between devices, body(): lax.all_to_all(packed, 'tile', split_axis=0, concat_axis=0, tiled=True)  17 us
    dot_general x1, matrix products, body(): jnp.dot(trace_rows, table_both, precision=lax.Precision.HIGHEST, preferre...  16.4 us
    dot_general x1, matrix products, body(): lax.dot_general(spectra, table_both, (((1,), (1,)), ((), ())), precision=...  15.1 us
  transfers between devices with their start and end apart: 2, of which 1 were waited for; matrix products, arithmetic and copies ran while one was open for 14% of the time, Pallas kernels for 0%

commit v1 on v0

v1 whole, which is shorter than its diff:
```python
import math

import jax
import jax.numpy as jnp
import numpy as np
from jax import lax
from jax.experimental import pallas as pl
from jax.experimental.pallas import tpu as pltpu
from jax.sharding import Mesh
from jax.sharding import PartitionSpec as P

LANES = 128
RADIX = 8
VMEM = pl.BlockSpec(memory_space=pltpu.VMEM)
SMEM = pl.BlockSpec(memory_space=pltpu.SMEM)
PLANE = ("section", "y", "x")
COLUMN = ("z", "sub")


def halves(value):
    high = value.astype(jnp.bfloat16)
    low = (value - high.astype(jnp.float32)).astype(jnp.bfloat16)
    return high, low


def product(left_high, left_low, right_high, right_low):
    rows = left_high.shape[0]
    both = jnp.dot(
        jnp.concatenate([left_high, left_low], axis=0),
        right_high,
        preferred_element_type=jnp.float32,
    )
    cross = jnp.dot(left_high, right_low, preferred_element_type=jnp.float32)
    return both[:rows] + (both[rows:] + cross)


def pack_kernel(rows_hbm, lists_ref, out_ref, columns_ref, sems):
    blocks = rows_hbm.shape[0] // 8
    copies = []
    for j in range(8):
        copy = pltpu.make_async_copy(
            rows_hbm.at[:, j * LANES : (j + 1) * LANES], columns_ref.at[j], sems.at[j]
        )
        copy.start()
        copies.append(copy)
    for d in range(32):
        out_ref[d, 2 * blocks :, :] = lists_ref[...]
    for j in range(8):
        copies[j].wait()
        q, h = j // 2, j % 2
        for r in range(8):
            out_ref[4 * r + q, h * blocks : (h + 1) * blocks, :] = columns_ref[
                j, pl.ds(r, blocks, stride=8), :
            ]


def stack_kernel(got_ref, out_ref):
    sources, height, _ = got_ref.shape
    blocks = (height - 8) // 2
    tiles = 128
    tile_ids = lax.broadcasted_iota(jnp.int32, (tiles, LANES), 0).astype(jnp.float32)
    mixing, naming = [], []
    for g in range(sources // 4):
        lists = got_ref[4 * g, 2 * blocks :, :]
        for i in range(1, 4):
            lists = lists + got_ref[4 * g + i, 2 * blocks :, :]
        mix = jnp.zeros((tiles, LANES), jnp.float32)
        names = jnp.zeros((tiles, LANES), jnp.float32)
        for a in range(4):
            hit = lists[a : a + 1, :] == tile_ids
            mix = mix + jnp.where(hit, lists[4 + a : 5 + a, :], 0.0)
            names = names + jnp.where(hit, 1.0, 0.0)
        mixing.append(mix)
        naming.append(names)
    mix_high, mix_low = halves(jnp.concatenate(mixing, axis=1))
    samples = jnp.concatenate(
        [
            got_ref[:, h * blocks : (h + 1) * blocks, :].reshape(sources * blocks, LANES)
            for h in range(2)
        ],
        axis=1,
    )
    stacked = product(mix_high, mix_low, *halves(samples))
    named = naming[0]
    for names in naming[1:]:
        named = named + names
    counts = lax.dot_general(
        jnp.ones((8, LANES), jnp.bfloat16),
        named.astype(jnp.bfloat16),
        (((1,), (1,)), ((), ())),
        preferred_element_type=jnp.float32,
    )
    peers = out_ref.shape[0]
    per_plane = tiles // (peers // 2)
    for p in range(peers):
        first = (p // 2) * per_plane
        for h in range(2):
            out_ref[p, pl.ds(h, per_plane, stride=2), :] = stacked[
                first : first + per_plane, h * LANES : (h + 1) * LANES
            ]
        out_ref[p, 2 * per_plane :, :] = counts


def sum_kernel(got_ref, out_ref, counts_ref):
    total = got_ref[0]
    for p in range(1, got_ref.shape[0]):
        total = total + got_ref[p]
    rows = total.shape[0] - 8
    out_ref[:rows, :] = total[:rows]
    out_ref[rows:, :] = total[:rows]
    counts_ref[...] = total[rows:]


def image_kernel(
    tile_ref,
    stacked_ref,
    counts_ref,
    gain_ref,
    turn_cos_ref,
    turn_sin_ref,
    ahead_high_ref,
    ahead_low_ref,
    back_high_ref,
    back_low_ref,
    spread_ref,
    weights_hbm,
    out_ref,
    weights_ref,
    sem,
):
    copy = pltpu.make_async_copy(weights_hbm, weights_ref, sem)
    copy.start()
    samples = RADIX * LANES
    parts = [stacked_ref[pl.ds(j, 8, stride=RADIX), :] for j in range(RADIX)]
    angle = [2.0 * math.pi * j / RADIX for j in range(RADIX)]

    def weighted(terms, factors):
        total = None
        for term, factor in zip(terms, factors):
            if abs(factor) < 1e-9:
                continue
            if abs(factor - 1.0) < 1e-9:
                piece = term
            elif abs(factor + 1.0) < 1e-9:
                piece = -term
            else:
                piece = term * np.float32(factor)
            total = piece if total is None else total + piece
        return jnp.zeros_like(terms[0]) if total is None else total

    real_rows, imag_rows = [], []
    for k in range(RADIX):
        real = weighted(parts, [math.cos(angle[j * k % RADIX]) for j in range(RADIX)])
        imag = weighted(parts, [-math.sin(angle[j * k % RADIX]) for j in range(RADIX)])
        turn_cos = turn_cos_ref[k : k + 1, :]
        turn_sin = turn_sin_ref[k : k + 1, :]
        real_rows.append(real * turn_cos + imag * turn_sin)
        imag_rows.append(imag * turn_cos - real * turn_sin)
    waves = jnp.concatenate(
        [jnp.concatenate(real_rows, axis=0), jnp.concatenate(imag_rows, axis=0)], axis=1
    )
    spectra = product(*halves(waves), ahead_high_ref[...], ahead_low_ref[...])
    gains = jnp.concatenate(
        [jnp.broadcast_to(gain_ref[k : k + 1, :], (8, LANES)) for k in range(RADIX)], axis=0
    )
    spectra = spectra * jnp.concatenate([gains, gains], axis=1)
    waves = product(*halves(spectra), back_high_ref[...], back_low_ref[...])
    real_rows, imag_rows = [], []
    for k in range(RADIX):
        real = waves[8 * k : 8 * k + 8, :LANES]
        imag = waves[8 * k : 8 * k + 8, LANES:]
        turn_cos = turn_cos_ref[k : k + 1, :]
        turn_sin = turn_sin_ref[k : k + 1, :]
        real_rows.append(real * turn_cos - imag * turn_sin)
        imag_rows.append(imag * turn_cos + real * turn_sin)
    filtered = []
    for j in range(RADIX):
        filtered.append(
            weighted(
                real_rows + imag_rows,
                [math.cos(angle[j * k % RADIX]) for k in range(RADIX)]
                + [-math.sin(angle[j * k % RADIX]) for k in range(RADIX)],
            )
            * np.float32(1.0 / samples)
        )
    filtered = jnp.concatenate(filtered, axis=1)
    lane = lax.broadcasted_iota(jnp.int32, (1, LANES), 1)
    fold = jnp.sum(
        jnp.where(lane == tile_ref[0], counts_ref[0:1, :], 0.0), axis=1, keepdims=True
    )
    copy.wait()
    focused = product(*halves(filtered), *halves(weights_ref[...])) / jnp.sqrt(fold)
    focused_high, focused_low = halves(focused)
    spread_high, spread_low = halves(spread_ref[...])
    out_ref[...] = lax.dot_general(
        jnp.concatenate([focused_high, focused_high, focused_low], axis=0),
        jnp.concatenate([spread_high, spread_low, spread_high], axis=0),
        (((0,), (0,)), ((), ())),
        preferred_element_type=jnp.float32,
    )


def fourier_parts():
    lane = np.arange(LANES)
    turns = 2.0 * np.pi * np.arange(RADIX)[:, None] * lane[None, :] / (RADIX * LANES)
    angles = 2.0 * np.pi * (lane[:, None] * lane[None, :] % LANES) / LANES
    cosine, sine = np.cos(angles), np.sin(angles)
    ahead = np.block([[cosine, -sine], [sine, cosine]]).astype(np.float32)
    ahead_high = ahead.astype(jnp.bfloat16)
    ahead_low = (ahead - ahead_high.astype(np.float32)).astype(jnp.bfloat16)
    return (
        np.cos(turns).astype(np.float32),
        np.sin(turns).astype(np.float32),
        ahead_high,
        ahead_low,
        np.ascontiguousarray(ahead_high.T),
        np.ascontiguousarray(ahead_low.T),
    )


def body(traces, band_gain, aperture, taper, weights, spread):
    f32 = jnp.float32
    blocks, per_block, samples = traces.shape
    x_at = lax.axis_index("x")
    tile_at = (lax.axis_index("z") * 4 + lax.axis_index("y")) * 4 + x_at
    lists = jnp.concatenate([aperture.astype(f32).T, taper.T], axis=0)
    owner = jnp.arange(LANES, dtype=jnp.int32) // blocks
    lists = jnp.where((owner == x_at)[None, :], jnp.tile(lists, (1, LANES // blocks)), 0.0)
    sent = pl.pallas_call(
        pack_kernel,
        out_shape=jax.ShapeDtypeStruct((32, 2 * blocks + 8, LANES), f32),
        in_specs=[pl.BlockSpec(memory_space=pl.ANY), VMEM],
        out_specs=VMEM,
        scratch_shapes=[
            pltpu.VMEM((8, blocks * per_block, LANES), f32),
            pltpu.SemaphoreType.DMA((8,)),
        ],
        name="pack",
    )(traces.reshape(blocks * per_block, samples), lists)
    got = lax.all_to_all(sent, PLANE, 0, 0, tiled=True)
    sent = pl.pallas_call(
        stack_kernel,
        out_shape=jax.ShapeDtypeStruct((16, 40, LANES), f32),
        in_specs=[VMEM],
        out_specs=VMEM,
        name="stack",
    )(got)
    got = lax.all_to_all(sent, COLUMN, 0, 0, tiled=True)
    sent, counts = pl.pallas_call(
        sum_kernel,
        out_shape=(
            jax.ShapeDtypeStruct((64, LANES), f32),
            jax.ShapeDtypeStruct((8, LANES), f32),
        ),
        in_specs=[VMEM],
        out_specs=(VMEM, VMEM),
        name="sum",
    )(got)
    got = lax.all_to_all(sent.reshape(32, 2, LANES), PLANE, 0, 0, tiled=True)
    depth = weights.shape[2]
    image = pl.pallas_call(
        image_kernel,
        out_shape=jax.ShapeDtypeStruct((depth, spread.shape[2]), f32),
        in_specs=[SMEM] + [VMEM] * 10 + [pl.BlockSpec(memory_space=pl.ANY)],
        out_specs=VMEM,
        scratch_shapes=[pltpu.VMEM((samples, depth), f32), pltpu.SemaphoreType.DMA],
        name="image",
    )(
        tile_at.astype(jnp.int32).reshape(1),
        got.reshape(64, LANES),
        counts,
        band_gain.reshape(LANES, RADIX).T,
        *[jnp.asarray(part) for part in fourier_parts()],
        spread[0],
        weights[0],
    )
    return image[None]


def solution(mesh):
    fine = Mesh(mesh.devices.reshape(2, 8, 4, 4, 2), ("section", "z", "y", "x", "sub"))
    tile = ("z", "y", "x")
    everyone = ("section",) + tile + ("sub",)
    placed = (
        P(everyone, None, None),
        P(),
        P(everyone, None),
        P(everyone, None),
        P(tile, None, ("section", "sub")),
        P(tile, None, None),
    )
    return jax.shard_map(
        body,
        mesh=fine,
        in_specs=placed,
        out_specs=P(tile, ("section", "sub"), None),
        check_vma=False,
    )
```

time: 533 us -> 91.4 us (0.17); the launches traced: 525 us -> 89.7 us
  waiting for transfers between devices: 363 us -> 6.2 us
  matrix products: 40.4 us -> 0 us
  starting transfers between devices: 37.4 us -> 7.92 us
  other arithmetic: 28.3 us -> 1.98 us
  blocking collectives: 38.5 us -> 60.9 us
  local copies, waits for them, and re-layouts: 16.3 us -> 1.44 us
  Pallas kernels: 0 us -> 11.3 us
    all_to_all x2 -> x1, waiting for transfers between devices: 363 us -> 6.2 us  [body(): got = lax.all_to_all(sent.reshape(32, 2, LANES), PLANE, 0, 0, tiled=True)]
    all_to_all x0 -> x2, blocking collectives: none -> 60.9 us  [the longest x1 30.8 us: body(): got = lax.all_to_all(sent, COLUMN, 0, 0, tiled=True)]
    dot_general x6 -> x0, matrix products: 40.4 us -> none  [the longest x1 16.4 us: body(): jnp.dot(trace_rows, table_both, precision=lax.Precision.HIGHEST, preferre...]
    psum x1 -> x0, blocking collectives: 38.5 us -> none  [body(): lax.psum((local_sum, fold_local), ('section', 'sub'))]
    all_to_all x2 -> x1, starting transfers between devices: 37.4 us -> 7.92 us  [body(): got = lax.all_to_all(sent.reshape(32, 2, LANES), PLANE, 0, 0, tiled=True)]
    sin x1 -> x0, other arithmetic: 17.6 us -> none  [fourier_table(): return jnp.concatenate([jnp.cos(angles), jnp.sin(angles)], axis=1)]
    pallas_call x0 -> x4, Pallas kernels: none -> 11.3 us  [the longest x1 3.87 us: body(): pl.pallas_call(image_kernel, out_shape=jax.ShapeDtypeStruct((depth, sprea...]
    reduce_sum x4 -> x0, other arithmetic: 10.7 us -> none  [the longest x1 5.78 us: body(): local_sum = jnp.sum(received, axis=(0, 1))]
  transfers between devices with their start and end apart: 2 -> 1, of which waited for: 1 -> 1; matrix products, arithmetic and copies ran while one was open for 14% -> 1% of each run, Pallas kernels for 0% -> 0%
where the time goes in v1:
time: 91.4 us; the launch traced here: 89.7 us
  blocking collectives  60.9 us (67%)
  Pallas kernels  11.3 us (12%)
  starting transfers between devices  7.92 us (9%)
  waiting for transfers between devices  6.2 us (7%)
  other arithmetic  1.98 us (2%)
  local copies, waits for them, and re-layouts  1.44 us (2%)
    all_to_all x1, blocking collectives, body(): got = lax.all_to_all(sent, COLUMN, 0, 0, tiled=True)  30.8 us
    all_to_all x1, blocking collectives, body(): got = lax.all_to_all(sent, PLANE, 0, 0, tiled=True)  30.1 us
    all_to_all x1, starting transfers between devices, body(): got = lax.all_to_all(sent.reshape(32, 2, LANES), PLANE, 0, 0, tiled=True)  7.92 us
    all_to_all x1, waiting for transfers between devices, body(): got = lax.all_to_all(sent.reshape(32, 2, LANES), PLANE, 0, 0, tiled=True)  6.2 us
    pallas_call x1, Pallas kernels, body(): pl.pallas_call(image_kernel, out_shape=jax.ShapeDtypeStruct((depth, sprea...  3.87 us
    pallas_call x1, Pallas kernels, body(): pl.pallas_call(pack_kernel, out_shape=jax.ShapeDtypeStruct((32, 2 * block...  3.11 us
    pallas_call x1, Pallas kernels, body(): pl.pallas_call(stack_kernel, out_shape=jax.ShapeDtypeStruct((16, 40, LANE...  2.71 us
  transfers between devices with their start and end apart: 1, of which 1 were waited for; matrix products, arithmetic and copies ran while one was open for 1% of the time, Pallas kernels for 0%

profile of v1, /device:TPU:1, one launch (start us, length us, event | category | flops | bytes accessed | tf_op | source)
XLA Modules:
  0.0 89.7 jit_solution(13944898558244185177)
XLA Ops:
  0.0 0.7 convert_bitcast_fusion
  0.7 0.7 pad_maximum_fusion
  1.4 0.1 tile.10
  1.5 0.6 broadcast_select_fusion.lists_ref
  2.1 3.1 %pack.1 = f32[32,72,128]{2,1,0:T(8,128)} custom-call(f32[256,1024]{1,0:T(8,128)} %bitcast.12, f32[8,128]{1,0:T(8,128)} %broadcast_select_fusion.lists_ref), custom_call_target="tpu_custom_call" | custom-call | tf_op jit(solution)/shard_map/pack/pallas_call | solution.py:229
  5.2 30.1 %all_to_all.15.got_ref = f32[32,72,128]{2,1,0:T(8,128)} all-to-all(f32[32,72,128]{2,1,0:T(8,128)} %pack.1), channel_id=1, replica_groups=mesh['section'=2,'z'=8,'y'=4,'x'=4,'sub'=2] {'section','y','x'}, dimensions={0} | all-to-all | bytes 2359296 | tf_op jit(solution)/shard_map/all_to_all | solution.py:240
  35.2 0.0 copy-start.1
  35.2 2.7 %stack.1 = f32[16,40,128]{2,1,0:T(8,128)} custom-call(f32[32,72,128]{2,1,0:T(8,128)} %all_to_all.15.got_ref), custom_call_target="tpu_custom_call" | custom-call | tf_op jit(solution)/shard_map/stack/pallas_call | solution.py:241
  38.0 30.8 %all_to_all.16.got_ref = f32[16,40,128]{2,1,0:T(8,128)} all-to-all(f32[16,40,128]{2,1,0:T(8,128)} %stack.1), channel_id=1, replica_groups=mesh['section'=2,'z'=8,'y'=4,'x'=4,'sub'=2] {'z','sub'}, dimensions={0} | all-to-all | bytes 655360 | tf_op jit(solution)/shard_map/all_to_all | solution.py:248
  68.8 1.6 %sum.1 = (f32[64,128]{1,0:T(8,128)}, f32[8,128]{1,0:T(8,128)}) custom-call(f32[16,40,128]{2,1,0:T(8,128)} %all_to_all.16.got_ref), custom_call_target="tpu_custom_call" | custom-call | tf_op jit(solution)/shard_map/sum/pallas_call | solution.py:249
  70.4 7.9 %all-to-all-start.2 = ((f32[32,2,128]{2,1,0:T(2,128)}), f32[32,2,128]{2,1,0:T(2,128)S(1)}, u32[]{:S(2)}, u32[]{:S(2)}) async-start(f32[32,2,128]{2,1,0:T(2,128)} %bitcast.14), calls=%async_computation.2 | async-start | bytes 65536 | tf_op jit(solution)/shard_map/all_to_all | solution.py:259
  78.3 0.0 copy-done.1
  78.3 0.1 reshape.37
  78.4 0.7 copy.13
  79.1 6.2 %all-to-all-done.2 = f32[32,2,128]{2,1,0:T(2,128)S(1)} async-done(((f32[32,2,128]{2,1,0:T(2,128)}), f32[32,2,128]{2,1,0:T(2,128)S(1)}, u32[]{:S(2)}, u32[]{:S(2)}) %all-to-all-start.2) | async-done | bytes 32800 | tf_op jit(solution)/shard_map/all_to_all | solution.py:259
  85.3 0.0 copy-start
  85.3 0.6 copy-done
  85.9 3.9 %image.1 = f32[384,128]{1,0:T(8,128)} custom-call(s32[1]{0:T(128)} %bitcast.tile_ref, f32[64,128]{1,0:T(8,128)} %bitcast.13, f32[8,128]{1,0:T(8,128)} %get-tuple-element.8.counts_ref, f32[8,128]{1,0:T(8,128)} %bitcast.15, f32[8,128]{1,0:T(8,128)} %constant.48.clone.turn_cos_ref, f32[8,128]{1,0:T(8,128)} %constant.49.clone.turn_sin_ref, ...), custom_call_target="tpu_custom_call" | custom-call | tf_op jit(solution)/shard_map/image/pallas_call | solution.py:261
  (2 shorter events, 0.0 us)
Async XLA Ops:
  35.2 43.1 %copy-start.1 = (f32[1024]{0:T(1024)S(1)}, f32[1024]{0:T(1024)}, u32[]{:S(2)}) copy-start(f32[1024]{0:T(1024)} %param.13) | copy-start | bytes 12292
  70.4 14.9 %all-to-all-start.2 = ((f32[32,2,128]{2,1,0:T(2,128)}), f32[32,2,128]{2,1,0:T(2,128)S(1)}, u32[]{:S(2)}, u32[]{:S(2)}) async-start(f32[32,2,128]{2,1,0:T(2,128)} %bitcast.14), calls=%async_computation.2 | async-start | bytes 65536 | tf_op jit(solution)/shard_map/all_to_all | solution.py:259
  85.3 0.6 copy-start

commit v2 on v1

--- a/solution.py
+++ b/solution.py
@@ -13,8 +13,9 @@
 RADIX = 8
 VMEM = pl.BlockSpec(memory_space=pltpu.VMEM)
 SMEM = pl.BlockSpec(memory_space=pltpu.SMEM)
-PLANE = ("section", "y", "x")
-COLUMN = ("z", "sub")
+NEAR = ("section", "z_pair", "y", "x")
+FAR = ("z_far", "sub")
+MIB = 1 << 20
 
 
 def halves(value):
@@ -34,7 +35,7 @@
     return both[:rows] + (both[rows:] + cross)
 
 
-def pack_kernel(rows_hbm, lists_ref, out_ref, columns_ref, sems):
+def pack_kernel(x_ref, rows_hbm, aperture_ref, taper_ref, out_ref, columns_ref, sems):
     blocks = rows_hbm.shape[0] // 8
     copies = []
     for j in range(8):
@@ -43,72 +44,56 @@
         )
         copy.start()
         copies.append(copy)
-    for d in range(32):
-        out_ref[d, 2 * blocks :, :] = lists_ref[...]
+    lists = jnp.concatenate([aperture_ref[...].astype(jnp.float32), taper_ref[...]], axis=0)
+    lists = jnp.concatenate([lists] * (LANES // blocks), axis=1)
+    owner = lax.broadcasted_iota(jnp.int32, (8, LANES), 1) // blocks
+    lists = jnp.where(owner == x_ref[0], lists, 0.0)
+    for d in range(64):
+        out_ref[d, blocks:, :] = lists
     for j in range(8):
         copies[j].wait()
-        q, h = j // 2, j % 2
         for r in range(8):
-            out_ref[4 * r + q, h * blocks : (h + 1) * blocks, :] = columns_ref[
-                j, pl.ds(r, blocks, stride=8), :
-            ]
+            out_ref[8 * r + j, :blocks, :] = columns_ref[j, pl.ds(r, blocks, stride=8), :]
 
 
 def stack_kernel(got_ref, out_ref):
     sources, height, _ = got_ref.shape
-    blocks = (height - 8) // 2
+    blocks = height - 8
     tiles = 128
     tile_ids = lax.broadcasted_iota(jnp.int32, (tiles, LANES), 0).astype(jnp.float32)
-    mixing, naming = [], []
+    mixing, named = [], jnp.zeros((tiles, LANES), jnp.float32)
     for g in range(sources // 4):
-        lists = got_ref[4 * g, 2 * blocks :, :]
+        lists = got_ref[4 * g, blocks:, :]
         for i in range(1, 4):
-            lists = lists + got_ref[4 * g + i, 2 * blocks :, :]
+            lists = lists + got_ref[4 * g + i, blocks:, :]
         mix = jnp.zeros((tiles, LANES), jnp.float32)
-        names = jnp.zeros((tiles, LANES), jnp.float32)
         for a in range(4):
             hit = lists[a : a + 1, :] == tile_ids
-            mix = mix + jnp.where(hit, lists[4 + a : 5 + a, :], 0.0)
-            names = names + jnp.where(hit, 1.0, 0.0)
+            mix = jnp.where(hit, lists[4 + a : 5 + a, :], mix)
         mixing.append(mix)
-        naming.append(names)
+        named = named + jnp.where(mix > 0.0, 1.0, 0.0)
     mix_high, mix_low = halves(jnp.concatenate(mixing, axis=1))
-    samples = jnp.concatenate(
-        [
-            got_ref[:, h * blocks : (h + 1) * blocks, :].reshape(sources * blocks, LANES)
-            for h in range(2)
-        ],
-        axis=1,
-    )
+    samples = got_ref[:, :blocks, :].reshape(sources * blocks, LANES)
     stacked = product(mix_high, mix_low, *halves(samples))
-    named = naming[0]
-    for names in naming[1:]:
-        named = named + names
     counts = lax.dot_general(
         jnp.ones((8, LANES), jnp.bfloat16),
         named.astype(jnp.bfloat16),
         (((1,), (1,)), ((), ())),
         preferred_element_type=jnp.float32,
     )
-    peers = out_ref.shape[0]
-    per_plane = tiles // (peers // 2)
-    for p in range(peers):
-        first = (p // 2) * per_plane
-        for h in range(2):
-            out_ref[p, pl.ds(h, per_plane, stride=2), :] = stacked[
-                first : first + per_plane, h * LANES : (h + 1) * LANES
-            ]
-        out_ref[p, 2 * per_plane :, :] = counts
+    for p in range(out_ref.shape[0]):
+        first = (p // 2) * 32
+        out_ref[p, :32, :] = stacked[first : first + 32]
+        out_ref[p, 32:, :] = counts
 
 
 def sum_kernel(got_ref, out_ref, counts_ref):
     total = got_ref[0]
     for p in range(1, got_ref.shape[0]):
         total = total + got_ref[p]
-    rows = total.shape[0] - 8
-    out_ref[:rows, :] = total[:rows]
-    out_ref[rows:, :] = total[:rows]
-    counts_ref[...] = total[rows:]
+    out_ref[:32, :] = total[:32]
+    out_ref[32:, :] = total[:32]
+    counts_ref[...] = total[32:]
 
 
 def image_kernel(
@@ -118,10 +103,7 @@
     gain_ref,
     turn_cos_ref,
     turn_sin_ref,
-    ahead_high_ref,
-    ahead_low_ref,
-    back_high_ref,
-    back_low_ref,
+    table_ref,
     spread_ref,
     weights_hbm,
     out_ref,
@@ -159,12 +141,18 @@
     waves = jnp.concatenate(
         [jnp.concatenate(real_rows, axis=0), jnp.concatenate(imag_rows, axis=0)], axis=1
     )
-    spectra = product(*halves(waves), ahead_high_ref[...], ahead_low_ref[...])
+    ahead = halves(table_ref[...])
+    back = []
+    for part in ahead:
+        top = jnp.concatenate([part[:LANES, :LANES], part[LANES:, :LANES]], axis=1)
+        bottom = jnp.concatenate([part[:LANES, LANES:], part[LANES:, LANES:]], axis=1)
+        back.append(jnp.concatenate([top, bottom], axis=0))
+    spectra = product(*halves(waves), *ahead)
     gains = jnp.concatenate(
         [jnp.broadcast_to(gain_ref[k : k + 1, :], (8, LANES)) for k in range(RADIX)], axis=0
     )
     spectra = spectra * jnp.concatenate([gains, gains], axis=1)
-    waves = product(*halves(spectra), back_high_ref[...], back_low_ref[...])
+    waves = product(*halves(spectra), *back)
     real_rows, imag_rows = [], []
     for k in range(RADIX):
         real = waves[8 * k : 8 * k + 8, :LANES]
@@ -205,47 +193,42 @@
     turns = 2.0 * np.pi * np.arange(RADIX)[:, None] * lane[None, :] / (RADIX * LANES)
     angles = 2.0 * np.pi * (lane[:, None] * lane[None, :] % LANES) / LANES
     cosine, sine = np.cos(angles), np.sin(angles)
-    ahead = np.block([[cosine, -sine], [sine, cosine]]).astype(np.float32)
-    ahead_high = ahead.astype(jnp.bfloat16)
-    ahead_low = (ahead - ahead_high.astype(np.float32)).astype(jnp.bfloat16)
     return (
         np.cos(turns).astype(np.float32),
         np.sin(turns).astype(np.float32),
-        ahead_high,
-        ahead_low,
-        np.ascontiguousarray(ahead_high.T),
-        np.ascontiguousarray(ahead_low.T),
+        np.block([[cosine, -sine], [sine, cosine]]).astype(np.float32),
     )
 
 
 def body(traces, band_gain, aperture, taper, weights, spread):
     f32 = jnp.float32
     blocks, per_block, samples = traces.shape
+    depth = weights.shape[2]
     x_at = lax.axis_index("x")
-    tile_at = (lax.axis_index("z") * 4 + lax.axis_index("y")) * 4 + x_at
-    lists = jnp.concatenate([aperture.astype(f32).T, taper.T], axis=0)
-    owner = jnp.arange(LANES, dtype=jnp.int32) // blocks
-    lists = jnp.where((owner == x_at)[None, :], jnp.tile(lists, (1, LANES // blocks)), 0.0)
+    z_at = lax.axis_index("z_far") * 2 + lax.axis_index("z_pair")
+    tile_at = (z_at * 4 + lax.axis_index("y")) * 4 + x_at
     sent = pl.pallas_call(
         pack_kernel,
-        out_shape=jax.ShapeDtypeStruct((32, 2 * blocks + 8, LANES), f32),
-        in_specs=[pl.BlockSpec(memory_space=pl.ANY), VMEM],
+        out_shape=jax.ShapeDtypeStruct((64, blocks + 8, LANES), f32),
+        in_specs=[SMEM, pl.BlockSpec(memory_space=pltpu.HBM), VMEM, VMEM],
         out_specs=VMEM,
         scratch_shapes=[
             pltpu.VMEM((8, blocks * per_block, LANES), f32),
             pltpu.SemaphoreType.DMA((8,)),
         ],
+        compiler_params=pltpu.CompilerParams(vmem_limit_bytes=6 * MIB),
         name="pack",
-    )(traces.reshape(blocks * per_block, samples), lists)
-    got = lax.all_to_all(sent, PLANE, 0, 0, tiled=True)
+    )(x_at.reshape(1), traces.reshape(blocks * per_block, samples), aperture.T, taper.T)
+    got = lax.all_to_all(sent, NEAR, 0, 0, tiled=True)
     sent = pl.pallas_call(
         stack_kernel,
-        out_shape=jax.ShapeDtypeStruct((16, 40, LANES), f32),
+        out_shape=jax.ShapeDtypeStruct((8, 40, LANES), f32),
         in_specs=[VMEM],
         out_specs=VMEM,
+        compiler_params=pltpu.CompilerParams(vmem_limit_bytes=16 * MIB),
         name="stack",
     )(got)
-    got = lax.all_to_all(sent, COLUMN, 0, 0, tiled=True)
+    got = lax.all_to_all(sent, FAR, 0, 0, tiled=True)
     sent, counts = pl.pallas_call(
         sum_kernel,
         out_shape=(
@@ -254,19 +237,20 @@
         ),
         in_specs=[VMEM],
         out_specs=(VMEM, VMEM),
+        compiler_params=pltpu.CompilerParams(vmem_limit_bytes=2 * MIB),
         name="sum",
     )(got)
-    got = lax.all_to_all(sent.reshape(32, 2, LANES), PLANE, 0, 0, tiled=True)
-    depth = weights.shape[2]
+    got = lax.all_to_all(sent.reshape(64, 1, LANES), NEAR, 0, 0, tiled=True)
     image = pl.pallas_call(
         image_kernel,
         out_shape=jax.ShapeDtypeStruct((depth, spread.shape[2]), f32),
-        in_specs=[SMEM] + [VMEM] * 10 + [pl.BlockSpec(memory_space=pl.ANY)],
+        in_specs=[SMEM] + [VMEM] * 7 + [pl.BlockSpec(memory_space=pl.ANY)],
         out_specs=VMEM,
         scratch_shapes=[pltpu.VMEM((samples, depth), f32), pltpu.SemaphoreType.DMA],
+        compiler_params=pltpu.CompilerParams(vmem_limit_bytes=16 * MIB),
         name="image",
     )(
-        tile_at.astype(jnp.int32).reshape(1),
+        tile_at.reshape(1),
         got.reshape(64, LANES),
         counts,
         band_gain.reshape(LANES, RADIX).T,
@@ -278,8 +262,11 @@
 
 
 def solution(mesh):
-    fine = Mesh(mesh.devices.reshape(2, 8, 4, 4, 2), ("section", "z", "y", "x", "sub"))
-    tile = ("z", "y", "x")
+    fine = Mesh(
+        mesh.devices.reshape(2, 4, 2, 4, 4, 2),
+        ("section", "z_far", "z_pair", "y", "x", "sub"),
+    )
+    tile = ("z_far", "z_pair", "y", "x")
     everyone = ("section",) + tile + ("sub",)
     placed = (
         P(everyone, None, None),

time: 91.4 us -> 79.6 us (0.87); the launches traced: 89.7 us -> 79.3 us
  Pallas kernels: 11.3 us -> 3.74 us
  blocking collectives: 60.9 us -> 56.3 us
  other arithmetic: 1.98 us -> 0 us
  waiting for transfers between devices: 6.2 us -> 7.55 us
  local copies, waits for them, and re-layouts: 1.44 us -> 2.74 us
    all_to_all x2, blocking collectives: 60.9 us -> 56.3 us  [the longest x1 30.9 us: body(): got = lax.all_to_all(sent, NEAR, 0, 0, tiled=True)]
    pallas_call x2, Pallas kernels: 5.81 us -> 1.4 us  [the longest x1 0.89 us: body(): pl.pallas_call(stack_kernel, out_shape=jax.ShapeDtypeStruct((8, 40, LANES...]
    pallas_call x1, Pallas kernels: 3.87 us -> 1.71 us  [body(): pl.pallas_call(image_kernel, out_shape=jax.ShapeDtypeStruct((depth, sprea...]
    unnamed x4 -> x18, local copies, waits for them, and re-layouts: 0.61 us -> 2.61 us
    all_to_all x1, waiting for transfers between devices: 6.2 us -> 7.55 us  [body(): got = lax.all_to_all(sent.reshape(64, 1, LANES), NEAR, 0, 0, tiled=True)]
    pallas_call x1, Pallas kernels: 1.61 us -> 0.63 us  [body(): pl.pallas_call(sum_kernel, out_shape=(jax.ShapeDtypeStruct((64, LANES), f...]
  transfers between devices with their start and end apart: 1 -> 1, of which waited for: 1 -> 1; matrix products, arithmetic and copies ran while one was open for 1% -> 0% of each run, Pallas kernels for 0% -> 0%
where the time goes in v2:
time: 79.6 us; the launch traced here: 79.3 us
  blocking collectives  56.3 us (71%)
  starting transfers between devices  8.82 us (11%)
  waiting for transfers between devices  7.55 us (9%)
  Pallas kernels  3.74 us (5%)
  local copies, waits for them, and re-layouts  2.74 us (3%)
    all_to_all x1, blocking collectives, body(): got = lax.all_to_all(sent, NEAR, 0, 0, tiled=True)  30.9 us
    all_to_all x1, blocking collectives, body(): got = lax.all_to_all(sent, FAR, 0, 0, tiled=True)  25.4 us
    all_to_all x1, starting transfers between devices, body(): got = lax.all_to_all(sent.reshape(64, 1, LANES), NEAR, 0, 0, tiled=True)  8.82 us
    all_to_all x1, waiting for transfers between devices, body(): got = lax.all_to_all(sent.reshape(64, 1, LANES), NEAR, 0, 0, tiled=True)  7.55 us
    unnamed x18, local copies, waits for them, and re-layouts  2.61 us
    pallas_call x1, Pallas kernels, body(): pl.pallas_call(image_kernel, out_shape=jax.ShapeDtypeStruct((depth, sprea...  1.71 us
  transfers between devices with their start and end apart: 1, of which 1 were waited for; matrix products, arithmetic and copies ran while one was open for 0% of the time, Pallas kernels for 0%

profile of v2, /device:TPU:1, one launch (start us, length us, event | category | flops | bytes accessed | tf_op | source)
XLA Modules:
  0.0 79.3 jit_solution(4887278579283268740)
XLA Ops:
  0.0 0.0 copy-start.1
  0.0 1.2 %copy-done.1 = f32[32,8,1024]{2,1,0:T(8,128)S(1)} copy-done((f32[32,8,1024]{2,1,0:T(8,128)S(1)}, f32[32,8,1024]{2,1,0:T(8,128)}, u32[]{:S(2)}) %copy-start.1) | copy-done | bytes 1048600
  1.2 0.0 copy-start.6
  1.2 0.7 copy-done.6
  1.9 0.0 copy-start.7
  1.9 0.7 copy-done.7
  2.6 0.5 pack.1
  3.1 30.9 %all_to_all.15.got_ref = f32[64,40,128]{2,1,0:T(8,128)S(1)} all-to-all(f32[64,40,128]{2,1,0:T(8,128)S(1)} %pack.1), channel_id=1, replica_groups=mesh['section'=2,'z_far'=4,'z_pair'=2,'y'=4,'x'=4,'sub'=2] {'section','z..., dimensions={0} | all-to-all | bytes 2621440 | tf_op jit(solution)/shard_map/all_to_all | solution.py:222
  34.0 0.0 copy-start.8
  34.0 0.0 copy-start
  34.0 0.0 copy-start.2
  34.0 0.0 copy-start.3
  34.0 0.0 copy-start.4
  34.0 0.0 copy-start.5
  34.1 0.9 %stack.1 = f32[8,40,128]{2,1,0:T(8,128)S(1)} custom-call(f32[64,40,128]{2,1,0:T(8,128)S(1)} %all_to_all.15.got_ref), custom_call_target="tpu_custom_call" | custom-call | tf_op jit(solution)/shard_map/stack/pallas_call | solution.py:223
  34.9 25.4 %all_to_all.16.got_ref = f32[8,40,128]{2,1,0:T(8,128)S(1)} all-to-all(f32[8,40,128]{2,1,0:T(8,128)S(1)} %stack.1), channel_id=1, replica_groups=mesh['section'=2,'z_far'=4,'z_pair'=2,'y'=4,'x'=4,'sub'=2] {'z_far','sub'}, dimensions={0} | all-to-all | bytes 327680 | tf_op jit(solution)/shard_map/all_to_all | solution.py:231
  60.4 0.6 sum.1
  61.0 8.8 %all-to-all-start.2 = ((f32[64,1,128]{2,1,0:T(1,128)}), f32[64,1,128]{2,1,0:T(1,128)S(1)}, u32[]{:S(2)}, u32[]{:S(2)}) async-start(f32[64,1,128]{2,1,0:T(1,128)} %bitcast.6), calls=%async_computation.2 | async-start | bytes 65536 | tf_op jit(solution)/shard_map/all_to_all | solution.py:243
  69.9 0.0 copy-done.8
  69.9 0.1 reshape.23
  70.0 7.6 %all-to-all-done.2 = f32[64,1,128]{2,1,0:T(1,128)S(1)} async-done(((f32[64,1,128]{2,1,0:T(1,128)}), f32[64,1,128]{2,1,0:T(1,128)S(1)}, u32[]{:S(2)}, u32[]{:S(2)}) %all-to-all-start.2) | async-done | bytes 32800 | tf_op jit(solution)/shard_map/all_to_all | solution.py:243
  77.5 0.0 copy-done
  77.6 0.0 copy-done.2
  77.6 0.0 copy-done.3
  77.6 0.0 copy-done.4
  77.6 0.0 copy-done.5
  77.6 1.7 %image.1 = f32[384,128]{1,0:T(8,128)} custom-call(s32[1]{0:T(128)} %bitcast.tile_ref, f32[64,128]{1,0:T(8,128)S(1)} %bitcast.15, f32[8,128]{1,0:T(8,128)S(1)} %get-tuple-element.8.counts_ref, f32[8,128]{1,0:T(8,128)S(1)} %bitcast.16, f32[8,128]{1,0:T(8,128)S(1)} %copy-done.4, f32[8,128]{1,0:T(8,128)S(1)} %copy-done.5, f32[256,256]{1,0:T(8,128)S(1)} %copy-done.2, ...), custom_call_target="tpu_custom_call" | custom-call | tf_op jit(solution)/shard_map/image/pallas_call | solution.py:244
  (1 shorter events, 0.0 us)
Async XLA Ops:
  0.0 1.2 %copy-start.1 = (f32[32,8,1024]{2,1,0:T(8,128)S(1)}, f32[32,8,1024]{2,1,0:T(8,128)}, u32[]{:S(2)}) copy-start(f32[32,8,1024]{2,1,0:T(8,128)} %param.9) | copy-start | bytes 3145732
  1.2 0.7 copy-start.6
  1.9 0.7 copy-start.7
  34.0 35.8 %copy-start.8 = (f32[1024]{0:T(1024)S(1)}, f32[1024]{0:T(1024)}, u32[]{:S(2)}) copy-start(f32[1024]{0:T(1024)} %param.10) | copy-start | bytes 12292
  34.0 43.5 %copy-start = (f32[1,1024,384]{2,1,0:T(8,128)S(1)}, f32[1,1024,384]{2,1,0:T(8,128)}, u32[]{:S(2)}) copy-start(f32[1,1024,384]{2,1,0:T(8,128)} %param.13) | copy-start | bytes 4718596
  34.0 43.5 %copy-start.2 = (f32[256,256]{1,0:T(8,128)S(1)}, f32[256,256]{1,0:T(8,128)}, u32[]{:S(2)}) copy-start(f32[256,256]{1,0:T(8,128)} %constant.29.clone.table_ref) | copy-start | bytes 786436
  34.0 43.5 %copy-start.3 = (f32[1,8,128]{2,1,0:T(8,128)S(1)}, f32[1,8,128]{2,1,0:T(8,128)}, u32[]{:S(2)}) copy-start(f32[1,8,128]{2,1,0:T(8,128)} %param.14) | copy-start | bytes 12292
  34.0 43.5 %copy-start.4 = (f32[8,128]{1,0:T(8,128)S(1)}, f32[8,128]{1,0:T(8,128)}, u32[]{:S(2)}) copy-start(f32[8,128]{1,0:T(8,128)} %constant.27.clone.turn_cos_ref) | copy-start | bytes 12292
  34.0 43.5 %copy-start.5 = (f32[8,128]{1,0:T(8,128)S(1)}, f32[8,128]{1,0:T(8,128)}, u32[]{:S(2)}) copy-start(f32[8,128]{1,0:T(8,128)} %constant.28.clone.turn_sin_ref) | copy-start | bytes 12292
  61.0 16.5 %all-to-all-start.2 = ((f32[64,1,128]{2,1,0:T(1,128)}), f32[64,1,128]{2,1,0:T(1,128)S(1)}, u32[]{:S(2)}, u32[]{:S(2)}) async-start(f32[64,1,128]{2,1,0:T(1,128)} %bitcast.6), calls=%async_computation.2 | async-start | bytes 65536 | tf_op jit(solution)/shard_map/all_to_all | solution.py:243

commit v3 on v2

--- a/solution.py
+++ b/solution.py
@@ -35,7 +35,7 @@
     return both[:rows] + (both[rows:] + cross)
 
 
-def pack_kernel(x_ref, rows_hbm, aperture_ref, taper_ref, out_ref, columns_ref, sems):
+def pack_kernel(x_ref, rows_hbm, lists_ref, out_ref, columns_ref, sems):
     blocks = rows_hbm.shape[0] // 8
     copies = []
     for j in range(8):
@@ -44,36 +44,54 @@
         )
         copy.start()
         copies.append(copy)
-    lists = jnp.concatenate([aperture_ref[...].astype(jnp.float32), taper_ref[...]], axis=0)
-    lists = jnp.concatenate([lists] * (LANES // blocks), axis=1)
-    owner = lax.broadcasted_iota(jnp.int32, (8, LANES), 1) // blocks
-    lists = jnp.where(owner == x_ref[0], lists, 0.0)
+    lists = jnp.concatenate([lists_ref[0], lists_ref[1]], axis=0)
+    lists = jnp.concatenate([lists] * 4, axis=1)
+    entry = lax.broadcasted_iota(jnp.int32, (8, LANES), 0) + x_ref[0]
+    lane = lax.broadcasted_iota(jnp.int32, (8, LANES), 1)
+    lists = jnp.where(lane // blocks == entry % 4, lists, 0.0)
+    lists = jnp.concatenate(
+        [jnp.sum(lists[4 * i : 4 * i + 4], axis=0, keepdims=True) for i in range(2)], axis=0
+    )
+    height = blocks + 2
     for d in range(64):
-        out_ref[d, blocks:, :] = lists
+        out_ref[height * d + blocks : height * (d + 1), :] = lists
     for j in range(8):
         copies[j].wait()
         for r in range(8):
-            out_ref[8 * r + j, :blocks, :] = columns_ref[j, pl.ds(r, blocks, stride=8), :]
+            first = height * (8 * r + j)
+            out_ref[first : first + blocks, :] = columns_ref[j, pl.ds(r, blocks, stride=8), :]
 
 
 def stack_kernel(got_ref, out_ref):
-    sources, height, _ = got_ref.shape
-    blocks = height - 8
-    tiles = 128
+    sources, blocks, tiles = 64, 32, 128
+    height = blocks + 2
     tile_ids = lax.broadcasted_iota(jnp.int32, (tiles, LANES), 0).astype(jnp.float32)
+    row = lax.broadcasted_iota(jnp.int32, (8, LANES), 0)
+    lane = lax.broadcasted_iota(jnp.int32, (8, LANES), 1)
+    own = lane // blocks == row % 4
+
+    def entries(offset, first, a):
+        rows = got_ref[pl.ds(height * first + offset, 8, stride=height), :]
+        rows = rows if a == 0 else pltpu.roll(rows, LANES - blocks * a, axis=1)
+        rows = jnp.where(own, rows, 0.0)
+        rows = rows + pltpu.roll(rows, 1, axis=0)
+        return rows + pltpu.roll(rows, 2, axis=0)
+
     mixing, named = [], jnp.zeros((tiles, LANES), jnp.float32)
-    for g in range(sources // 4):
-        lists = got_ref[4 * g, blocks:, :]
-        for i in range(1, 4):
-            lists = lists + got_ref[4 * g + i, blocks:, :]
-        mix = jnp.zeros((tiles, LANES), jnp.float32)
-        for a in range(4):
-            hit = lists[a : a + 1, :] == tile_ids
-            mix = jnp.where(hit, lists[4 + a : 5 + a, :], mix)
-        mixing.append(mix)
-        named = named + jnp.where(mix > 0.0, 1.0, 0.0)
+    for first in range(0, sources, 8):
+        apertures = [entries(blocks, first, a) for a in range(4)]
+        tapers = [entries(blocks + 1, first, a) for a in range(4)]
+        for at in (3, 7):
+            mix = jnp.zeros((tiles, LANES), jnp.float32)
+            for a in range(4):
+                hit = apertures[a][at : at + 1, :] == tile_ids
+                mix = jnp.where(hit, tapers[a][at : at + 1, :], mix)
+            mixing.append(mix)
+            named = named + jnp.where(mix > 0.0, 1.0, 0.0)
     mix_high, mix_low = halves(jnp.concatenate(mixing, axis=1))
-    samples = got_ref[:, :blocks, :].reshape(sources * blocks, LANES)
+    samples = jnp.concatenate(
+        [got_ref[height * s : height * s + blocks, :] for s in range(sources)], axis=0
+    )
     stacked = product(mix_high, mix_low, *halves(samples))
     counts = lax.dot_general(
         jnp.ones((8, LANES), jnp.bfloat16),
@@ -81,19 +99,20 @@
         (((1,), (1,)), ((), ())),
         preferred_element_type=jnp.float32,
     )
-    for p in range(out_ref.shape[0]):
+    for p in range(8):
         first = (p // 2) * 32
-        out_ref[p, :32, :] = stacked[first : first + 32]
-        out_ref[p, 32:, :] = counts
+        out_ref[33 * p : 33 * p + 32, :] = stacked[first : first + 32]
+        out_ref[33 * p + 32 : 33 * p + 33, :] = counts[:1]
 
 
 def sum_kernel(got_ref, out_ref, counts_ref):
-    total = got_ref[0]
-    for p in range(1, got_ref.shape[0]):
-        total = total + got_ref[p]
-    out_ref[:32, :] = total[:32]
-    out_ref[32:, :] = total[:32]
-    counts_ref[...] = total[32:]
+    total, counts = got_ref[:32, :], got_ref[32:33, :]
+    for p in range(1, 8):
+        total = total + got_ref[33 * p : 33 * p + 32, :]
+        counts = counts + got_ref[33 * p + 32 : 33 * p + 33, :]
+    out_ref[:32, :] = total
+    out_ref[32:, :] = total
+    counts_ref[...] = counts
 
 
 def image_kernel(
@@ -207,10 +226,13 @@
     x_at = lax.axis_index("x")
     z_at = lax.axis_index("z_far") * 2 + lax.axis_index("z_pair")
     tile_at = (z_at * 4 + lax.axis_index("y")) * 4 + x_at
+    lists = jnp.where(
+        jnp.arange(2)[:, None, None] == 0, aperture.T.astype(f32)[None], taper.T[None]
+    )
     sent = pl.pallas_call(
         pack_kernel,
-        out_shape=jax.ShapeDtypeStruct((64, blocks + 8, LANES), f32),
-        in_specs=[SMEM, pl.BlockSpec(memory_space=pltpu.HBM), VMEM, VMEM],
+        out_shape=jax.ShapeDtypeStruct((64 * (blocks + 2), LANES), f32),
+        in_specs=[SMEM, pl.BlockSpec(memory_space=pl.ANY), VMEM],
         out_specs=VMEM,
         scratch_shapes=[
             pltpu.VMEM((8, blocks * per_block, LANES), f32),
@@ -218,28 +240,28 @@
         ],
         compiler_params=pltpu.CompilerParams(vmem_limit_bytes=6 * MIB),
         name="pack",
-    )(x_at.reshape(1), traces.reshape(blocks * per_block, samples), aperture.T, taper.T)
-    got = lax.all_to_all(sent, NEAR, 0, 0, tiled=True)
+    )(x_at.reshape(1), traces.reshape(blocks * per_block, samples), lists)
+    got = lax.all_to_all(sent.reshape(64, -1, 2, LANES), NEAR, 0, 0, tiled=True)
     sent = pl.pallas_call(
         stack_kernel,
-        out_shape=jax.ShapeDtypeStruct((8, 40, LANES), f32),
+        out_shape=jax.ShapeDtypeStruct((8 * 33, LANES), f32),
         in_specs=[VMEM],
         out_specs=VMEM,
         compiler_params=pltpu.CompilerParams(vmem_limit_bytes=16 * MIB),
         name="stack",
-    )(got)
-    got = lax.all_to_all(sent, FAR, 0, 0, tiled=True)
+    )(got.reshape(-1, LANES))
+    got = lax.all_to_all(sent.reshape(8, 33, 1, LANES), FAR, 0, 0, tiled=True)
     sent, counts = pl.pallas_call(
         sum_kernel,
         out_shape=(
             jax.ShapeDtypeStruct((64, LANES), f32),
-            jax.ShapeDtypeStruct((8, LANES), f32),
+            jax.ShapeDtypeStruct((1, LANES), f32),
         ),
         in_specs=[VMEM],
         out_specs=(VMEM, VMEM),
         compiler_params=pltpu.CompilerParams(vmem_limit_bytes=2 * MIB),
         name="sum",
-    )(got)
+    )(got.reshape(-1, LANES))
     got = lax.all_to_all(sent.reshape(64, 1, LANES), NEAR, 0, 0, tiled=True)
     image = pl.pallas_call(
         image_kernel,

time: 79.6 us -> 77 us (0.967)
  blocking collectives: 56.3 us -> 54.2 us
  other arithmetic: 0 us -> 1.44 us
  local copies, waits for them, and re-layouts: 2.74 us -> 1.38 us
    all_to_all x2, blocking collectives: 56.3 us -> 54.2 us  [the longest x1 28.9 us: body(): got = lax.all_to_all(sent.reshape(64, -1, 2, LANES), NEAR, 0, 0, tiled=True)]
    unnamed x18 -> x14, local copies, waits for them, and re-layouts: 2.61 us -> 1.25 us
where the time goes in v3:
time: 77 us; the launch traced here: 76.7 us
  blocking collectives  54.2 us (70%)
  starting transfers between devices  8.23 us (11%)
  waiting for transfers between devices  7.55 us (10%)
  Pallas kernels  3.8 us (5%)
  other arithmetic  1.44 us (2%)
  local copies, waits for them, and re-layouts  1.38 us (2%)
    all_to_all x1, blocking collectives, body(): got = lax.all_to_all(sent.reshape(64, -1, 2, LANES), NEAR, 0, 0, tiled=True)  28.9 us
    all_to_all x1, blocking collectives, body(): got = lax.all_to_all(sent.reshape(8, 33, 1, LANES), FAR, 0, 0, tiled=True)  25.2 us
    all_to_all x1, starting transfers between devices, body(): got = lax.all_to_all(sent.reshape(64, 1, LANES), NEAR, 0, 0, tiled=True)  8.23 us
    all_to_all x1, waiting for transfers between devices, body(): got = lax.all_to_all(sent.reshape(64, 1, LANES), NEAR, 0, 0, tiled=True)  7.55 us
    pallas_call x1, Pallas kernels, body(): pl.pallas_call(image_kernel, out_shape=jax.ShapeDtypeStruct((depth, sprea...  1.71 us
  transfers between devices with their start and end apart: 1, of which 1 were waited for; matrix products, arithmetic and copies ran while one was open for 0% of the time, Pallas kernels for 0%

profile of v3, /device:TPU:1, one launch (start us, length us, event | category | flops | bytes accessed | tf_op | source)
XLA Modules:
  0.0 76.7 jit_solution(6802987379931126745)
XLA Ops:
  0.0 0.7 convert_bitcast_fusion
  0.7 0.8 broadcast_select_fusion.lists_ref
  1.4 0.0 copy-start.1
  1.4 1.2 %copy-done.1 = f32[32,8,1024]{2,1,0:T(8,128)S(1)} copy-done((f32[32,8,1024]{2,1,0:T(8,128)S(1)}, f32[32,8,1024]{2,1,0:T(8,128)}, u32[]{:S(2)}) %copy-start.1) | copy-done | bytes 1048600
  2.7 0.5 pack.1
  3.2 0.0 copy-start.6
  3.2 28.9 %all_to_all.15 = f32[64,17,2,128]{3,2,1,0:T(2,128)S(1)} all-to-all(f32[64,17,2,128]{3,2,1,0:T(2,128)S(1)} %bitcast.18), channel_id=1, replica_groups=mesh['section'=2,'z_far'=4,'z_pair'=2,'y'=4,'x'=4,'sub'=2] {'section','z..., dimensions={0} | all-to-all | bytes 2228224 | tf_op jit(solution)/shard_map/all_to_all | solution.py:244
  32.1 0.0 copy-start
  32.1 0.0 copy-start.2
  32.1 0.0 copy-start.3
  32.1 0.0 copy-start.4
  32.1 0.0 copy-start.5
  32.2 0.9 %stack.1 = f32[264,128]{1,0:T(8,128)S(1)} custom-call(f32[2176,128]{1,0:T(8,128)S(1)} %bitcast.19), custom_call_target="tpu_custom_call" | custom-call | tf_op jit(solution)/shard_map/stack/pallas_call | solution.py:245
  33.1 25.2 %all_to_all.16 = f32[8,33,1,128]{3,2,1,0:T(1,128)S(1)} all-to-all(f32[8,33,1,128]{3,2,1,0:T(1,128)S(1)} %bitcast.22), channel_id=1, replica_groups=mesh['section'=2,'z_far'=4,'z_pair'=2,'y'=4,'x'=4,'sub'=2] {'z_far','sub'}, dimensions={0} | all-to-all | bytes 270336 | tf_op jit(solution)/shard_map/all_to_all | solution.py:253
  58.4 0.6 sum.1
  59.0 8.2 %all-to-all-start.2 = ((f32[64,1,128]{2,1,0:T(1,128)}), f32[64,1,128]{2,1,0:T(1,128)S(1)}, u32[]{:S(2)}, u32[]{:S(2)}) async-start(f32[64,1,128]{2,1,0:T(1,128)} %bitcast.10), calls=%async_computation.2 | async-start | bytes 65536 | tf_op jit(solution)/shard_map/all_to_all | solution.py:265
  67.2 0.0 copy-done.6
  67.2 0.1 reshape.46
  67.4 7.6 %all-to-all-done.2 = f32[64,1,128]{2,1,0:T(1,128)S(1)} async-done(((f32[64,1,128]{2,1,0:T(1,128)}), f32[64,1,128]{2,1,0:T(1,128)S(1)}, u32[]{:S(2)}, u32[]{:S(2)}) %all-to-all-start.2) | async-done | bytes 32800 | tf_op jit(solution)/shard_map/all_to_all | solution.py:265
  74.9 0.0 copy-done
  74.9 0.0 copy-done.2
  74.9 0.0 copy-done.3
  74.9 0.0 copy-done.4
  75.0 0.0 copy-done.5
  75.0 1.7 %image.1 = f32[384,128]{1,0:T(8,128)} custom-call(s32[1]{0:T(128)} %bitcast.tile_ref, f32[64,128]{1,0:T(8,128)S(1)} %bitcast.24, f32[1,128]{1,0:T(1,128)S(1)} %get-tuple-element.8.counts_ref, f32[8,128]{1,0:T(8,128)S(1)} %bitcast.25, f32[8,128]{1,0:T(8,128)S(1)} %copy-done.4, f32[8,128]{1,0:T(8,128)S(1)} %copy-done.5, f32[256,256]{1,0:T(8,128)S(1)} %copy-done.2, ...), custom_call_target="tpu_custom_call" | custom-call | tf_op jit(solution)/shard_map/image/pallas_call | solution.py:266
  (2 shorter events, 0.1 us)
Async XLA Ops:
  1.4 1.2 %copy-start.1 = (f32[32,8,1024]{2,1,0:T(8,128)S(1)}, f32[32,8,1024]{2,1,0:T(8,128)}, u32[]{:S(2)}) copy-start(f32[32,8,1024]{2,1,0:T(8,128)} %param.9) | copy-start | bytes 3145732
  3.2 64.0 %copy-start.6 = (f32[1024]{0:T(1024)S(1)}, f32[1024]{0:T(1024)}, u32[]{:S(2)}) copy-start(f32[1024]{0:T(1024)} %param.10) | copy-start | bytes 12292
  32.1 42.8 %copy-start = (f32[1,1024,384]{2,1,0:T(8,128)S(1)}, f32[1,1024,384]{2,1,0:T(8,128)}, u32[]{:S(2)}) copy-start(f32[1,1024,384]{2,1,0:T(8,128)} %param.13) | copy-start | bytes 4718596
  32.1 42.8 %copy-start.2 = (f32[256,256]{1,0:T(8,128)S(1)}, f32[256,256]{1,0:T(8,128)}, u32[]{:S(2)}) copy-start(f32[256,256]{1,0:T(8,128)} %constant.31.clone.table_ref) | copy-start | bytes 786436
  32.1 42.8 %copy-start.3 = (f32[1,8,128]{2,1,0:T(8,128)S(1)}, f32[1,8,128]{2,1,0:T(8,128)}, u32[]{:S(2)}) copy-start(f32[1,8,128]{2,1,0:T(8,128)} %param.14) | copy-start | bytes 12292
  32.1 42.8 %copy-start.4 = (f32[8,128]{1,0:T(8,128)S(1)}, f32[8,128]{1,0:T(8,128)}, u32[]{:S(2)}) copy-start(f32[8,128]{1,0:T(8,128)} %constant.29.clone.turn_cos_ref) | copy-start | bytes 12292
  32.1 42.8 %copy-start.5 = (f32[8,128]{1,0:T(8,128)S(1)}, f32[8,128]{1,0:T(8,128)}, u32[]{:S(2)}) copy-start(f32[8,128]{1,0:T(8,128)} %constant.30.clone.turn_sin_ref) | copy-start | bytes 12292
  59.0 16.0 %all-to-all-start.2 = ((f32[64,1,128]{2,1,0:T(1,128)}), f32[64,1,128]{2,1,0:T(1,128)S(1)}, u32[]{:S(2)}, u32[]{:S(2)}) async-start(f32[64,1,128]{2,1,0:T(1,128)} %bitcast.10), calls=%async_computation.2 | async-start | bytes 65536 | tf_op jit(solution)/shard_map/all_to_all | solution.py:265

commit v4 on v3

--- a/solution.py
+++ b/solution.py
@@ -11,10 +11,18 @@
 
 LANES = 128
 RADIX = 8
+HBM = pl.BlockSpec(memory_space=pl.ANY)
 VMEM = pl.BlockSpec(memory_space=pltpu.VMEM)
 SMEM = pl.BlockSpec(memory_space=pltpu.SMEM)
-NEAR = ("section", "z_pair", "y", "x")
+NEAR = ("section", "y", "x", "z_pair")
+SPREAD_FIRST = 63
+GATHER_FIRST = 63
+SPREAD_ORDER = [(SPREAD_FIRST + i) % 64 for i in range(64)]
+GATHER_ORDER = [(GATHER_FIRST + i) % 64 for i in range(64)]
 FAR = ("z_far", "sub")
+FAR_ORDER = [1, 0, 3, 2, 5, 4, 7, 6]
+TILE = ("z_far", "z_pair", "y", "x")
+SIZES = {"section": 2, "z_pair": 2, "y": 4, "x": 4}
 MIB = 1 << 20
 
 
@@ -35,18 +43,40 @@
     return both[:rows] + (both[rows:] + cross)
 
 
-def pack_kernel(x_ref, rows_hbm, lists_ref, out_ref, columns_ref, sems):
+def in_hbm(array):
+    return pltpu.with_memory_space_constraint(array, pltpu.HBM)
+
+
+def pack_kernel(
+    place_ref,
+    rows_hbm,
+    aperture_hbm,
+    taper_hbm,
+    out_ref,
+    columns_ref,
+    aperture_ref,
+    taper_ref,
+    sems,
+    list_sems,
+):
     blocks = rows_hbm.shape[0] // 8
-    copies = []
+    copies = [
+        pltpu.make_async_copy(aperture_hbm, aperture_ref, list_sems.at[0]),
+        pltpu.make_async_copy(taper_hbm, taper_ref, list_sems.at[1]),
+    ]
+    for copy in copies:
+        copy.start()
     for j in range(8):
         copy = pltpu.make_async_copy(
             rows_hbm.at[:, j * LANES : (j + 1) * LANES], columns_ref.at[j], sems.at[j]
         )
         copy.start()
         copies.append(copy)
-    lists = jnp.concatenate([lists_ref[0], lists_ref[1]], axis=0)
+    copies.pop(0).wait()
+    copies.pop(0).wait()
+    lists = jnp.concatenate([aperture_ref[...].astype(jnp.float32), taper_ref[...]], axis=0)
     lists = jnp.concatenate([lists] * 4, axis=1)
-    entry = lax.broadcasted_iota(jnp.int32, (8, LANES), 0) + x_ref[0]
+    entry = lax.broadcasted_iota(jnp.int32, (8, LANES), 0) + place_ref[0]
     lane = lax.broadcasted_iota(jnp.int32, (8, LANES), 1)
     lists = jnp.where(lane // blocks == entry % 4, lists, 0.0)
     lists = jnp.concatenate(
@@ -58,7 +88,7 @@
     for j in range(8):
         copies[j].wait()
         for r in range(8):
-            first = height * (8 * r + j)
+            first = height * SPREAD_ORDER.index(GATHER_ORDER[8 * r + j])
             out_ref[first : first + blocks, :] = columns_ref[j, pl.ds(r, blocks, stride=8), :]
 
 
@@ -100,9 +130,18 @@
         preferred_element_type=jnp.float32,
     )
     for p in range(8):
-        first = (p // 2) * 32
+        first = (FAR_ORDER[p] // 2) * 32
         out_ref[33 * p : 33 * p + 32, :] = stacked[first : first + 32]
         out_ref[33 * p + 32 : 33 * p + 33, :] = counts[:1]
+
+
+def near_tiles():
+    owners = []
+    places = list(np.ndindex(*[SIZES[axis] for axis in NEAR]))
+    for index in GATHER_ORDER:
+        at = dict(zip(NEAR, places[index]))
+        owners.append((at["z_pair"] * 4 + at["y"]) * 4 + at["x"])
+    return owners
 
 
 def sum_kernel(got_ref, out_ref, counts_ref):
@@ -110,8 +149,8 @@
     for p in range(1, 8):
         total = total + got_ref[33 * p : 33 * p + 32, :]
         counts = counts + got_ref[33 * p + 32 : 33 * p + 33, :]
-    out_ref[:32, :] = total
-    out_ref[32:, :] = total
+    for d, owner in enumerate(near_tiles()):
+        out_ref[d : d + 1, :] = total[owner : owner + 1]
     counts_ref[...] = counts
 
 
@@ -223,25 +262,30 @@
     f32 = jnp.float32
     blocks, per_block, samples = traces.shape
     depth = weights.shape[2]
-    x_at = lax.axis_index("x")
-    z_at = lax.axis_index("z_far") * 2 + lax.axis_index("z_pair")
-    tile_at = (z_at * 4 + lax.axis_index("y")) * 4 + x_at
-    lists = jnp.where(
-        jnp.arange(2)[:, None, None] == 0, aperture.T.astype(f32)[None], taper.T[None]
-    )
+    tile_at = lax.axis_index(TILE)
     sent = pl.pallas_call(
         pack_kernel,
         out_shape=jax.ShapeDtypeStruct((64 * (blocks + 2), LANES), f32),
-        in_specs=[SMEM, pl.BlockSpec(memory_space=pl.ANY), VMEM],
+        in_specs=[SMEM, HBM, HBM, HBM],
         out_specs=VMEM,
         scratch_shapes=[
             pltpu.VMEM((8, blocks * per_block, LANES), f32),
+            pltpu.VMEM((4, blocks), jnp.int32),
+            pltpu.VMEM((4, blocks), f32),
             pltpu.SemaphoreType.DMA((8,)),
+            pltpu.SemaphoreType.DMA((2,)),
         ],
         compiler_params=pltpu.CompilerParams(vmem_limit_bytes=6 * MIB),
         name="pack",
-    )(x_at.reshape(1), traces.reshape(blocks * per_block, samples), lists)
-    got = lax.all_to_all(sent.reshape(64, -1, 2, LANES), NEAR, 0, 0, tiled=True)
+    )(
+        ((lax.axis_index(NEAR) - SPREAD_FIRST) % 4).reshape(1),
+        in_hbm(traces.reshape(blocks * per_block, samples)),
+        in_hbm(aperture.T),
+        in_hbm(taper.T),
+    )
+    got = lax.all_to_all(
+        sent.reshape(64, -1, 2, LANES), NEAR, 0, 0, axis_index_groups=[SPREAD_ORDER], tiled=True
+    )
     sent = pl.pallas_call(
         stack_kernel,
         out_shape=jax.ShapeDtypeStruct((8 * 33, LANES), f32),
@@ -250,7 +294,9 @@
         compiler_params=pltpu.CompilerParams(vmem_limit_bytes=16 * MIB),
         name="stack",
     )(got.reshape(-1, LANES))
-    got = lax.all_to_all(sent.reshape(8, 33, 1, LANES), FAR, 0, 0, tiled=True)
+    got = lax.all_to_all(
+        sent.reshape(8, 33, 1, LANES), FAR, 0, 0, axis_index_groups=[FAR_ORDER], tiled=True
+    )
     sent, counts = pl.pallas_call(
         sum_kernel,
         out_shape=(
@@ -262,7 +308,9 @@
         compiler_params=pltpu.CompilerParams(vmem_limit_bytes=2 * MIB),
         name="sum",
     )(got.reshape(-1, LANES))
-    got = lax.all_to_all(sent.reshape(64, 1, LANES), NEAR, 0, 0, tiled=True)
+    got = lax.all_to_all(
+        sent.reshape(64, 1, LANES), NEAR, 0, 0, axis_index_groups=[GATHER_ORDER], tiled=True
+    )
     image = pl.pallas_call(
         image_kernel,
         out_shape=jax.ShapeDtypeStruct((depth, spread.shape[2]), f32),
@@ -288,20 +336,19 @@
         mesh.devices.reshape(2, 4, 2, 4, 4, 2),
         ("section", "z_far", "z_pair", "y", "x", "sub"),
     )
-    tile = ("z_far", "z_pair", "y", "x")
-    everyone = ("section",) + tile + ("sub",)
+    everyone = ("section",) + TILE + ("sub",)
     placed = (
         P(everyone, None, None),
         P(),
         P(everyone, None),
         P(everyone, None),
-        P(tile, None, ("section", "sub")),
-        P(tile, None, None),
+        P(TILE, None, ("section", "sub")),
+        P(TILE, None, None),
     )
     return jax.shard_map(
         body,
         mesh=fine,
         in_specs=placed,
-        out_specs=P(tile, ("section", "sub"), None),
+        out_specs=P(TILE, ("section", "sub"), None),
         check_vma=False,
     )

time: 77 us -> 66.5 us (0.86)
  blocking collectives: 54.2 us -> 47.7 us
  waiting for transfers between devices: 7.55 us -> 3.18 us
  starting transfers between devices: 8.23 us -> 10.4 us
  other arithmetic: 1.44 us -> 0 us
  local copies, waits for them, and re-layouts: 1.38 us -> 0.16 us
  Pallas kernels: 3.8 us -> 4.76 us
    all_to_all x2, blocking collectives: 54.2 us -> 47.7 us  [the longest x1 28.6 us: body(): lax.all_to_all(sent.reshape(64, -1, 2, LANES), NEAR, 0, 0, axis_index_gro...]
    all_to_all x1, waiting for transfers between devices: 7.55 us -> 3.18 us  [body(): lax.all_to_all(sent.reshape(64, 1, LANES), NEAR, 0, 0, axis_index_groups=...]
    all_to_all x1, starting transfers between devices: 8.23 us -> 10.4 us  [body(): lax.all_to_all(sent.reshape(64, 1, LANES), NEAR, 0, 0, axis_index_groups=...]
    unnamed x14 -> x12, local copies, waits for them, and re-layouts: 1.25 us -> 0.03 us
    pallas_call x1, Pallas kernels: 0.52 us -> 1.48 us  [body(): pl.pallas_call(pack_kernel, out_shape=jax.ShapeDtypeStruct((64 * (blocks...]
where the time goes in v4:
time: 66.5 us; the launch traced here: 66.2 us
  blocking collectives  47.7 us (72%)
  starting transfers between devices  10.4 us (16%)
  Pallas kernels  4.76 us (7%)
  waiting for transfers between devices  3.18 us (5%)
    all_to_all x1, blocking collectives, body(): lax.all_to_all(sent.reshape(64, -1, 2, LANES), NEAR, 0, 0, axis_index_gro...  28.6 us
    all_to_all x1, blocking collectives, body(): lax.all_to_all(sent.reshape(8, 33, 1, LANES), FAR, 0, 0, axis_index_group...  19.1 us
    all_to_all x1, starting transfers between devices, body(): lax.all_to_all(sent.reshape(64, 1, LANES), NEAR, 0, 0, axis_index_groups=...  10.4 us
    all_to_all x1, waiting for transfers between devices, body(): lax.all_to_all(sent.reshape(64, 1, LANES), NEAR, 0, 0, axis_index_groups=...  3.18 us
    pallas_call x1, Pallas kernels, body(): pl.pallas_call(image_kernel, out_shape=jax.ShapeDtypeStruct((depth, sprea...  1.71 us
    pallas_call x1, Pallas kernels, body(): pl.pallas_call(pack_kernel, out_shape=jax.ShapeDtypeStruct((64 * (blocks...  1.48 us
  transfers between devices with their start and end apart: 1, of which 1 were waited for; matrix products, arithmetic and copies ran while one was open for 0% of the time, Pallas kernels for 0%

profile of v4, /device:TPU:1, one launch (start us, length us, event | category | flops | bytes accessed | tf_op | source)
XLA Modules:
  0.0 66.2 jit_solution(852785153122213568)
XLA Ops:
  0.0 1.5 %pack.1 = f32[2176,128]{1,0:T(8,128)S(1)} custom-call(s32[1]{0:T(128)} %bitcast.1.place_ref, f32[256,1024]{1,0:T(8,128)} %bitcast.25, s32[4,32]{1,0:T(4,128)} %bitcast.26, f32[4,32]{1,0:T(4,128)} %bitcast.27), custom_call_target="tpu_custom_call" | custom-call | tf_op jit(solution)/shard_map/pack/pallas_call | solution.py:266
  1.5 0.0 copy-start.5
  1.5 28.6 %all_to_all.15 = f32[64,17,2,128]{3,2,1,0:T(2,128)S(1)} all-to-all(f32[64,17,2,128]{3,2,1,0:T(2,128)S(1)} %bitcast.17), channel_id=1, replica_groups={{318,0,32,2,34,4,36,6,38,8,40,10,42,12,44,14,46,16,48,18,50,20,52,22,54..., dimensions={0} | all-to-all | bytes 2228224 | tf_op jit(solution)/shard_map/all_to_all | solution.py:286
  30.1 0.0 copy-start
  30.1 0.0 copy-start.1
  30.1 0.0 copy-start.2
  30.1 0.0 copy-start.3
  30.1 0.0 copy-start.4
  30.1 0.9 %stack.1 = f32[264,128]{1,0:T(8,128)S(1)} custom-call(f32[2176,128]{1,0:T(8,128)S(1)} %bitcast.18), custom_call_target="tpu_custom_call" | custom-call | tf_op jit(solution)/shard_map/stack/pallas_call | solution.py:289
  31.1 19.1 %all_to_all.16 = f32[8,33,1,128]{3,2,1,0:T(1,128)S(1)} all-to-all(f32[8,33,1,128]{3,2,1,0:T(1,128)S(1)} %bitcast.20), channel_id=1, replica_groups={{1,0,65,64,129,128,193,192},{3,2,67,66,131,130,195,194},{5,4,69,68,133,..., dimensions={0} | all-to-all | bytes 270336 | tf_op jit(solution)/shard_map/all_to_all | solution.py:297
  50.1 0.6 sum.1
  50.8 10.4 %all-to-all-start.2 = ((f32[64,1,128]{2,1,0:T(1,128)}), f32[64,1,128]{2,1,0:T(1,128)S(1)}, u32[]{:S(2)}, u32[]{:S(2)}) async-start(f32[64,1,128]{2,1,0:T(1,128)} %bitcast.10), calls=%async_computation.2 | async-start | bytes 65536 | tf_op jit(solution)/shard_map/all_to_all | solution.py:311
  61.2 0.0 copy-done.5
  61.2 0.1 reshape.39
  61.3 3.2 %all-to-all-done.2 = f32[64,1,128]{2,1,0:T(1,128)S(1)} async-done(((f32[64,1,128]{2,1,0:T(1,128)}), f32[64,1,128]{2,1,0:T(1,128)S(1)}, u32[]{:S(2)}, u32[]{:S(2)}) %all-to-all-start.2) | async-done | bytes 32800 | tf_op jit(solution)/shard_map/all_to_all | solution.py:311
  64.5 0.0 copy-done
  64.5 0.0 copy-done.1
  64.5 0.0 copy-done.2
  64.5 0.0 copy-done.3
  64.5 0.0 copy-done.4
  64.5 1.7 %image.1 = f32[384,128]{1,0:T(8,128)} custom-call(s32[1]{0:T(128)} %bitcast.tile_ref, f32[64,128]{1,0:T(8,128)S(1)} %bitcast.22, f32[1,128]{1,0:T(1,128)S(1)} %get-tuple-element.8.counts_ref, f32[8,128]{1,0:T(8,128)S(1)} %bitcast.23, f32[8,128]{1,0:T(8,128)S(1)} %copy-done.3, f32[8,128]{1,0:T(8,128)S(1)} %copy-done.4, f32[256,256]{1,0:T(8,128)S(1)} %copy-done.1, ...), custom_call_target="tpu_custom_call" | custom-call | tf_op jit(solution)/shard_map/image/pallas_call | solution.py:314
  (1 shorter events, 0.0 us)
Async XLA Ops:
  1.5 59.7 %copy-start.5 = (f32[1024]{0:T(1024)S(1)}, f32[1024]{0:T(1024)}, u32[]{:S(2)}) copy-start(f32[1024]{0:T(1024)} %param.10) | copy-start | bytes 12292
  30.1 34.4 %copy-start = (f32[1,1024,384]{2,1,0:T(8,128)S(1)}, f32[1,1024,384]{2,1,0:T(8,128)}, u32[]{:S(2)}) copy-start(f32[1,1024,384]{2,1,0:T(8,128)} %param.13) | copy-start | bytes 4718596
  30.1 34.4 %copy-start.1 = (f32[256,256]{1,0:T(8,128)S(1)}, f32[256,256]{1,0:T(8,128)}, u32[]{:S(2)}) copy-start(f32[256,256]{1,0:T(8,128)} %constant.53.clone.table_ref) | copy-start | bytes 786436
  30.1 34.4 %copy-start.2 = (f32[1,8,128]{2,1,0:T(8,128)S(1)}, f32[1,8,128]{2,1,0:T(8,128)}, u32[]{:S(2)}) copy-start(f32[1,8,128]{2,1,0:T(8,128)} %param.14) | copy-start | bytes 12292
  30.1 34.4 %copy-start.3 = (f32[8,128]{1,0:T(8,128)S(1)}, f32[8,128]{1,0:T(8,128)}, u32[]{:S(2)}) copy-start(f32[8,128]{1,0:T(8,128)} %constant.51.clone.turn_cos_ref) | copy-start | bytes 12292
  30.1 34.4 %copy-start.4 = (f32[8,128]{1,0:T(8,128)S(1)}, f32[8,128]{1,0:T(8,128)}, u32[]{:S(2)}) copy-start(f32[8,128]{1,0:T(8,128)} %constant.52.clone.turn_sin_ref) | copy-start | bytes 12292
  50.8 13.7 %all-to-all-start.2 = ((f32[64,1,128]{2,1,0:T(1,128)}), f32[64,1,128]{2,1,0:T(1,128)S(1)}, u32[]{:S(2)}, u32[]{:S(2)}) async-start(f32[64,1,128]{2,1,0:T(1,128)} %bitcast.10), calls=%async_computation.2 | async-start | bytes 65536 | tf_op jit(solution)/shard_map/all_to_all | solution.py:311

commit v5 on v4

--- a/solution.py
+++ b/solution.py
@@ -20,7 +20,7 @@
 SPREAD_ORDER = [(SPREAD_FIRST + i) % 64 for i in range(64)]
 GATHER_ORDER = [(GATHER_FIRST + i) % 64 for i in range(64)]
 FAR = ("z_far", "sub")
-FAR_ORDER = [1, 0, 3, 2, 5, 4, 7, 6]
+FAR_ORDER = [1, 0, 2, 4, 6, 7, 5, 3]
 TILE = ("z_far", "z_pair", "y", "x")
 SIZES = {"section": 2, "z_pair": 2, "y": 4, "x": 4}
 MIB = 1 << 20

time: 66.5 us -> 66.8 us (level)
  blocking collectives: 47.7 us -> 49.5 us
  starting transfers between devices: 10.4 us -> 8.87 us
    all_to_all x1, blocking collectives: 19.1 us -> 21 us  [body(): lax.all_to_all(sent.reshape(8, 33, 1, LANES), FAR, 0, 0, axis_index_group...]
    all_to_all x1, starting transfers between devices: 10.4 us -> 8.87 us  [body(): lax.all_to_all(sent.reshape(64, 1, LANES), NEAR, 0, 0, axis_index_groups=...]
where the time goes in v5:
time: 66.8 us; the launch traced here: 66.6 us
  blocking collectives  49.5 us (74%)
  starting transfers between devices  8.87 us (13%)
  Pallas kernels  4.76 us (7%)
  waiting for transfers between devices  3.18 us (5%)
    all_to_all x1, blocking collectives, body(): lax.all_to_all(sent.reshape(64, -1, 2, LANES), NEAR, 0, 0, axis_index_gro...  28.6 us
    all_to_all x1, blocking collectives, body(): lax.all_to_all(sent.reshape(8, 33, 1, LANES), FAR, 0, 0, axis_index_group...  21 us
    all_to_all x1, starting transfers between devices, body(): lax.all_to_all(sent.reshape(64, 1, LANES), NEAR, 0, 0, axis_index_groups=...  8.87 us
    all_to_all x1, waiting for transfers between devices, body(): lax.all_to_all(sent.reshape(64, 1, LANES), NEAR, 0, 0, axis_index_groups=...  3.18 us
    pallas_call x1, Pallas kernels, body(): pl.pallas_call(image_kernel, out_shape=jax.ShapeDtypeStruct((depth, sprea...  1.71 us
    pallas_call x1, Pallas kernels, body(): pl.pallas_call(pack_kernel, out_shape=jax.ShapeDtypeStruct((64 * (blocks...  1.48 us
  transfers between devices with their start and end apart: 1, of which 1 were waited for; matrix products, arithmetic and copies ran while one was open for 0% of the time, Pallas kernels for 0%

profile of v5, /device:TPU:1, one launch (start us, length us, event | category | flops | bytes accessed | tf_op | source)
XLA Modules:
  0.0 66.6 jit_solution(4115183723798127053)
XLA Ops:
  0.0 1.5 %pack.1 = f32[2176,128]{1,0:T(8,128)S(1)} custom-call(s32[1]{0:T(128)} %bitcast.1.place_ref, f32[256,1024]{1,0:T(8,128)} %bitcast.25, s32[4,32]{1,0:T(4,128)} %bitcast.26, f32[4,32]{1,0:T(4,128)} %bitcast.27), custom_call_target="tpu_custom_call" | custom-call | tf_op jit(solution)/shard_map/pack/pallas_call | solution.py:266
  1.5 0.0 copy-start.5
  1.5 28.6 %all_to_all.15 = f32[64,17,2,128]{3,2,1,0:T(2,128)S(1)} all-to-all(f32[64,17,2,128]{3,2,1,0:T(2,128)S(1)} %bitcast.17), channel_id=1, replica_groups={{318,0,32,2,34,4,36,6,38,8,40,10,42,12,44,14,46,16,48,18,50,20,52,22,54..., dimensions={0} | all-to-all | bytes 2228224 | tf_op jit(solution)/shard_map/all_to_all | solution.py:286
  30.1 0.0 copy-start
  30.1 0.0 copy-start.1
  30.1 0.0 copy-start.2
  30.1 0.0 copy-start.3
  30.1 0.0 copy-start.4
  30.1 0.9 %stack.1 = f32[264,128]{1,0:T(8,128)S(1)} custom-call(f32[2176,128]{1,0:T(8,128)S(1)} %bitcast.18), custom_call_target="tpu_custom_call" | custom-call | tf_op jit(solution)/shard_map/stack/pallas_call | solution.py:289
  31.1 21.0 %all_to_all.16 = f32[8,33,1,128]{3,2,1,0:T(1,128)S(1)} all-to-all(f32[8,33,1,128]{3,2,1,0:T(1,128)S(1)} %bitcast.20), channel_id=1, replica_groups={{1,0,64,128,192,193,129,65},{3,2,66,130,194,195,131,67},{5,4,68,132,196..., dimensions={0} | all-to-all | bytes 270336 | tf_op jit(solution)/shard_map/all_to_all | solution.py:297
  52.0 0.6 sum.1
  52.6 8.9 %all-to-all-start.2 = ((f32[64,1,128]{2,1,0:T(1,128)}), f32[64,1,128]{2,1,0:T(1,128)S(1)}, u32[]{:S(2)}, u32[]{:S(2)}) async-start(f32[64,1,128]{2,1,0:T(1,128)} %bitcast.10), calls=%async_computation.2 | async-start | bytes 65536 | tf_op jit(solution)/shard_map/all_to_all | solution.py:311
  61.5 0.0 copy-done.5
  61.5 0.1 reshape.39
  61.7 3.2 %all-to-all-done.2 = f32[64,1,128]{2,1,0:T(1,128)S(1)} async-done(((f32[64,1,128]{2,1,0:T(1,128)}), f32[64,1,128]{2,1,0:T(1,128)S(1)}, u32[]{:S(2)}, u32[]{:S(2)}) %all-to-all-start.2) | async-done | bytes 32800 | tf_op jit(solution)/shard_map/all_to_all | solution.py:311
  64.9 0.0 copy-done
  64.9 0.0 copy-done.1
  64.9 0.0 copy-done.2
  64.9 0.0 copy-done.3
  64.9 0.0 copy-done.4
  64.9 1.7 %image.1 = f32[384,128]{1,0:T(8,128)} custom-call(s32[1]{0:T(128)} %bitcast.tile_ref, f32[64,128]{1,0:T(8,128)S(1)} %bitcast.22, f32[1,128]{1,0:T(1,128)S(1)} %get-tuple-element.8.counts_ref, f32[8,128]{1,0:T(8,128)S(1)} %bitcast.23, f32[8,128]{1,0:T(8,128)S(1)} %copy-done.3, f32[8,128]{1,0:T(8,128)S(1)} %copy-done.4, f32[256,256]{1,0:T(8,128)S(1)} %copy-done.1, ...), custom_call_target="tpu_custom_call" | custom-call | tf_op jit(solution)/shard_map/image/pallas_call | solution.py:314
  (1 shorter events, 0.0 us)
Async XLA Ops:
  1.5 60.0 %copy-start.5 = (f32[1024]{0:T(1024)S(1)}, f32[1024]{0:T(1024)}, u32[]{:S(2)}) copy-start(f32[1024]{0:T(1024)} %param.10) | copy-start | bytes 12292
  30.1 34.8 %copy-start = (f32[1,1024,384]{2,1,0:T(8,128)S(1)}, f32[1,1024,384]{2,1,0:T(8,128)}, u32[]{:S(2)}) copy-start(f32[1,1024,384]{2,1,0:T(8,128)} %param.13) | copy-start | bytes 4718596
  30.1 34.8 %copy-start.1 = (f32[256,256]{1,0:T(8,128)S(1)}, f32[256,256]{1,0:T(8,128)}, u32[]{:S(2)}) copy-start(f32[256,256]{1,0:T(8,128)} %constant.53.clone.table_ref) | copy-start | bytes 786436
  30.1 34.8 %copy-start.2 = (f32[1,8,128]{2,1,0:T(8,128)S(1)}, f32[1,8,128]{2,1,0:T(8,128)}, u32[]{:S(2)}) copy-start(f32[1,8,128]{2,1,0:T(8,128)} %param.14) | copy-start | bytes 12292
  30.1 34.8 %copy-start.3 = (f32[8,128]{1,0:T(8,128)S(1)}, f32[8,128]{1,0:T(8,128)}, u32[]{:S(2)}) copy-start(f32[8,128]{1,0:T(8,128)} %constant.51.clone.turn_cos_ref) | copy-start | bytes 12292
  30.1 34.8 %copy-start.4 = (f32[8,128]{1,0:T(8,128)S(1)}, f32[8,128]{1,0:T(8,128)}, u32[]{:S(2)}) copy-start(f32[8,128]{1,0:T(8,128)} %constant.52.clone.turn_sin_ref) | copy-start | bytes 12292
  52.6 12.2 %all-to-all-start.2 = ((f32[64,1,128]{2,1,0:T(1,128)}), f32[64,1,128]{2,1,0:T(1,128)S(1)}, u32[]{:S(2)}, u32[]{:S(2)}) async-start(f32[64,1,128]{2,1,0:T(1,128)} %bitcast.10), calls=%async_computation.2 | async-start | bytes 65536 | tf_op jit(solution)/shard_map/all_to_all | solution.py:311

commit v6 on v4

--- a/solution.py
+++ b/solution.py
@@ -15,7 +15,7 @@
 VMEM = pl.BlockSpec(memory_space=pltpu.VMEM)
 SMEM = pl.BlockSpec(memory_space=pltpu.SMEM)
 NEAR = ("section", "y", "x", "z_pair")
-SPREAD_FIRST = 63
+SPREAD_FIRST = 53
 GATHER_FIRST = 63
 SPREAD_ORDER = [(SPREAD_FIRST + i) % 64 for i in range(64)]
 GATHER_ORDER = [(GATHER_FIRST + i) % 64 for i in range(64)]
@@ -45,6 +45,10 @@
 
 def in_hbm(array):
     return pltpu.with_memory_space_constraint(array, pltpu.HBM)
+
+
+def in_vmem(array):
+    return pltpu.with_memory_space_constraint(array, pltpu.VMEM)
 
 
 def pack_kernel(
@@ -163,13 +167,9 @@
     turn_sin_ref,
     table_ref,
     spread_ref,
-    weights_hbm,
+    weights_ref,
     out_ref,
-    weights_ref,
-    sem,
 ):
-    copy = pltpu.make_async_copy(weights_hbm, weights_ref, sem)
-    copy.start()
     samples = RADIX * LANES
     parts = [stacked_ref[pl.ds(j, 8, stride=RADIX), :] for j in range(RADIX)]
     angle = [2.0 * math.pi * j / RADIX for j in range(RADIX)]
@@ -234,7 +234,6 @@
     fold = jnp.sum(
         jnp.where(lane == tile_ref[0], counts_ref[0:1, :], 0.0), axis=1, keepdims=True
     )
-    copy.wait()
     focused = product(*halves(filtered), *halves(weights_ref[...])) / jnp.sqrt(fold)
     focused_high, focused_low = halves(focused)
     spread_high, spread_low = halves(spread_ref[...])
@@ -314,9 +313,8 @@
     image = pl.pallas_call(
         image_kernel,
         out_shape=jax.ShapeDtypeStruct((depth, spread.shape[2]), f32),
-        in_specs=[SMEM] + [VMEM] * 7 + [pl.BlockSpec(memory_space=pl.ANY)],
+        in_specs=[SMEM] + [VMEM] * 8,
         out_specs=VMEM,
-        scratch_shapes=[pltpu.VMEM((samples, depth), f32), pltpu.SemaphoreType.DMA],
         compiler_params=pltpu.CompilerParams(vmem_limit_bytes=16 * MIB),
         name="image",
     )(

time: 66.5 us -> 66.1 us (level)
  blocking collectives: 47.7 us -> 47 us
where the time goes in v6:
time: 66.1 us; the launch traced here: 65.9 us
  blocking collectives  47 us (71%)
  starting transfers between devices  10.8 us (16%)
  Pallas kernels  4.64 us (7%)
  waiting for transfers between devices  3.18 us (5%)
    all_to_all x1, blocking collectives, body(): lax.all_to_all(sent.reshape(64, -1, 2, LANES), NEAR, 0, 0, axis_index_gro...  27.9 us
    all_to_all x1, blocking collectives, body(): lax.all_to_all(sent.reshape(8, 33, 1, LANES), FAR, 0, 0, axis_index_group...  19 us
    all_to_all x1, starting transfers between devices, body(): lax.all_to_all(sent.reshape(64, 1, LANES), NEAR, 0, 0, axis_index_groups=...  10.8 us
    all_to_all x1, waiting for transfers between devices, body(): lax.all_to_all(sent.reshape(64, 1, LANES), NEAR, 0, 0, axis_index_groups=...  3.18 us
    pallas_call x1, Pallas kernels, body(): pl.pallas_call(image_kernel, out_shape=jax.ShapeDtypeStruct((depth, sprea...  1.6 us
    pallas_call x1, Pallas kernels, body(): pl.pallas_call(pack_kernel, out_shape=jax.ShapeDtypeStruct((64 * (blocks...  1.48 us
  transfers between devices with their start and end apart: 1, of which 1 were waited for; matrix products, arithmetic and copies ran while one was open for 0% of the time, Pallas kernels for 0%

profile of v6, /device:TPU:1, one launch (start us, length us, event | category | flops | bytes accessed | tf_op | source)
XLA Modules:
  0.0 65.9 jit_solution(14307822823902426972)
XLA Ops:
  0.0 1.5 %pack.1 = f32[2176,128]{1,0:T(8,128)S(1)} custom-call(s32[1]{0:T(128)} %bitcast.1.place_ref, f32[256,1024]{1,0:T(8,128)} %bitcast.25, s32[4,32]{1,0:T(4,128)} %bitcast.26, f32[4,32]{1,0:T(4,128)} %bitcast.27), custom_call_target="tpu_custom_call" | custom-call | tf_op jit(solution)/shard_map/pack/pallas_call | solution.py:265
  1.5 0.0 copy-start.5
  1.5 27.9 %all_to_all.15 = f32[64,17,2,128]{3,2,1,0:T(2,128)S(1)} all-to-all(f32[64,17,2,128]{3,2,1,0:T(2,128)S(1)} %bitcast.17), channel_id=1, replica_groups={{308,278,310,280,312,282,314,284,316,286,318,0,32,2,34,4,36,6,38,8,40,1..., dimensions={0} | all-to-all | bytes 2228224 | tf_op jit(solution)/shard_map/all_to_all | solution.py:285
  29.4 0.0 copy-start
  29.4 0.0 copy-start.1
  29.4 0.0 copy-start.2
  29.4 0.0 copy-start.3
  29.4 0.0 copy-start.4
  29.4 0.9 %stack.1 = f32[264,128]{1,0:T(8,128)S(1)} custom-call(f32[2176,128]{1,0:T(8,128)S(1)} %bitcast.18), custom_call_target="tpu_custom_call" | custom-call | tf_op jit(solution)/shard_map/stack/pallas_call | solution.py:288
  30.4 19.0 %all_to_all.16 = f32[8,33,1,128]{3,2,1,0:T(1,128)S(1)} all-to-all(f32[8,33,1,128]{3,2,1,0:T(1,128)S(1)} %bitcast.20), channel_id=1, replica_groups={{1,0,65,64,129,128,193,192},{3,2,67,66,131,130,195,194},{5,4,69,68,133,..., dimensions={0} | all-to-all | bytes 270336 | tf_op jit(solution)/shard_map/all_to_all | solution.py:296
  49.4 0.6 sum.1
  50.1 10.8 %all-to-all-start.2 = ((f32[64,1,128]{2,1,0:T(1,128)}), f32[64,1,128]{2,1,0:T(1,128)S(1)}, u32[]{:S(2)}, u32[]{:S(2)}) async-start(f32[64,1,128]{2,1,0:T(1,128)} %bitcast.10), calls=%async_computation.2 | async-start | bytes 65536 | tf_op jit(solution)/shard_map/all_to_all | solution.py:310
  60.9 0.0 copy-done.5
  60.9 0.1 reshape.39
  61.1 3.2 %all-to-all-done.2 = f32[64,1,128]{2,1,0:T(1,128)S(1)} async-done(((f32[64,1,128]{2,1,0:T(1,128)}), f32[64,1,128]{2,1,0:T(1,128)S(1)}, u32[]{:S(2)}, u32[]{:S(2)}) %all-to-all-start.2) | async-done | bytes 32800 | tf_op jit(solution)/shard_map/all_to_all | solution.py:310
  64.2 0.0 copy-done
  64.2 0.0 copy-done.1
  64.2 0.0 copy-done.2
  64.2 0.0 copy-done.3
  64.3 0.0 copy-done.4
  64.3 1.6 %image.1 = f32[384,128]{1,0:T(8,128)} custom-call(s32[1]{0:T(128)} %bitcast.tile_ref, f32[64,128]{1,0:T(8,128)S(1)} %bitcast.22, f32[1,128]{1,0:T(1,128)S(1)} %get-tuple-element.8.counts_ref, f32[8,128]{1,0:T(8,128)S(1)} %bitcast.23, f32[8,128]{1,0:T(8,128)S(1)} %copy-done.3, f32[8,128]{1,0:T(8,128)S(1)} %copy-done.4, f32[256,256]{1,0:T(8,128)S(1)} %copy-done.1, ...), custom_call_target="tpu_custom_call" | custom-call | tf_op jit(solution)/shard_map/image/pallas_call | solution.py:313
  (1 shorter events, 0.0 us)
Async XLA Ops:
  1.5 59.4 %copy-start.5 = (f32[1024]{0:T(1024)S(1)}, f32[1024]{0:T(1024)}, u32[]{:S(2)}) copy-start(f32[1024]{0:T(1024)} %param.10) | copy-start | bytes 12292
  29.4 34.8 %copy-start = (f32[1,1024,384]{2,1,0:T(8,128)S(1)}, f32[1,1024,384]{2,1,0:T(8,128)}, u32[]{:S(2)}) copy-start(f32[1,1024,384]{2,1,0:T(8,128)} %param.13) | copy-start | bytes 4718596
  29.4 34.8 %copy-start.1 = (f32[256,256]{1,0:T(8,128)S(1)}, f32[256,256]{1,0:T(8,128)}, u32[]{:S(2)}) copy-start(f32[256,256]{1,0:T(8,128)} %constant.53.clone.table_ref) | copy-start | bytes 786436
  29.4 34.8 %copy-start.2 = (f32[1,8,128]{2,1,0:T(8,128)S(1)}, f32[1,8,128]{2,1,0:T(8,128)}, u32[]{:S(2)}) copy-start(f32[1,8,128]{2,1,0:T(8,128)} %param.14) | copy-start | bytes 12292
  29.4 34.8 %copy-start.3 = (f32[8,128]{1,0:T(8,128)S(1)}, f32[8,128]{1,0:T(8,128)}, u32[]{:S(2)}) copy-start(f32[8,128]{1,0:T(8,128)} %constant.51.clone.turn_cos_ref) | copy-start | bytes 12292
  29.4 34.8 %copy-start.4 = (f32[8,128]{1,0:T(8,128)S(1)}, f32[8,128]{1,0:T(8,128)}, u32[]{:S(2)}) copy-start(f32[8,128]{1,0:T(8,128)} %constant.52.clone.turn_sin_ref) | copy-start | bytes 12292
  50.1 14.2 %all-to-all-start.2 = ((f32[64,1,128]{2,1,0:T(1,128)}), f32[64,1,128]{2,1,0:T(1,128)S(1)}, u32[]{:S(2)}, u32[]{:S(2)}) async-start(f32[64,1,128]{2,1,0:T(1,128)} %bitcast.10), calls=%async_computation.2 | async-start | bytes 65536 | tf_op jit(solution)/shard_map/all_to_all | solution.py:310

commit v7 on v6

--- a/solution.py
+++ b/solution.py
@@ -20,7 +20,7 @@
 SPREAD_ORDER = [(SPREAD_FIRST + i) % 64 for i in range(64)]
 GATHER_ORDER = [(GATHER_FIRST + i) % 64 for i in range(64)]
 FAR = ("z_far", "sub")
-FAR_ORDER = [1, 0, 3, 2, 5, 4, 7, 6]
+FAR_ORDER = [3, 2, 1, 0, 5, 4, 7, 6]
 TILE = ("z_far", "z_pair", "y", "x")
 SIZES = {"section": 2, "z_pair": 2, "y": 4, "x": 4}
 MIB = 1 << 20
@@ -93,7 +93,13 @@
         copies[j].wait()
         for r in range(8):
             first = height * SPREAD_ORDER.index(GATHER_ORDER[8 * r + j])
-            out_ref[first : first + blocks, :] = columns_ref[j, pl.ds(r, blocks, stride=8), :]
+            at = 0
+            while at < blocks:
+                count = min(8 - (first + at) % 8, blocks - at)
+                out_ref[first + at : first + at + count, :] = columns_ref[
+                    j, pl.ds(r + 8 * at, count, stride=8), :
+                ]
+                at += count
 
 
 def stack_kernel(got_ref, out_ref):

time: 66.1 us -> 66 us (level)
  starting transfers between devices: 10.8 us -> 9.64 us
  blocking collectives: 47 us -> 48 us
    all_to_all x1, starting transfers between devices: 10.8 us -> 9.64 us  [body(): lax.all_to_all(sent.reshape(64, 1, LANES), NEAR, 0, 0, axis_index_groups=...]
    all_to_all x1, blocking collectives: 19 us -> 20.1 us  [body(): lax.all_to_all(sent.reshape(8, 33, 1, LANES), FAR, 0, 0, axis_index_group...]
where the time goes in v7:
time: 66 us; the launch traced here: 65.7 us
  blocking collectives  48 us (73%)
  starting transfers between devices  9.64 us (15%)
  Pallas kernels  4.66 us (7%)
  waiting for transfers between devices  3.18 us (5%)
    all_to_all x1, blocking collectives, body(): lax.all_to_all(sent.reshape(64, -1, 2, LANES), NEAR, 0, 0, axis_index_gro...  27.9 us
    all_to_all x1, blocking collectives, body(): lax.all_to_all(sent.reshape(8, 33, 1, LANES), FAR, 0, 0, axis_index_group...  20.1 us
    all_to_all x1, starting transfers between devices, body(): lax.all_to_all(sent.reshape(64, 1, LANES), NEAR, 0, 0, axis_index_groups=...  9.64 us
    all_to_all x1, waiting for transfers between devices, body(): lax.all_to_all(sent.reshape(64, 1, LANES), NEAR, 0, 0, axis_index_groups=...  3.18 us
    pallas_call x1, Pallas kernels, body(): pl.pallas_call(image_kernel, out_shape=jax.ShapeDtypeStruct((depth, sprea...  1.6 us
    pallas_call x1, Pallas kernels, body(): pl.pallas_call(pack_kernel, out_shape=jax.ShapeDtypeStruct((64 * (blocks...  1.49 us
  transfers between devices with their start and end apart: 1, of which 1 were waited for; matrix products, arithmetic and copies ran while one was open for 0% of the time, Pallas kernels for 0%

profile of v7, /device:TPU:1, one launch (start us, length us, event | category | flops | bytes accessed | tf_op | source)
XLA Modules:
  0.0 65.7 jit_solution(1399210766387897670)
XLA Ops:
  0.0 1.5 %pack.1 = f32[2176,128]{1,0:T(8,128)S(1)} custom-call(s32[1]{0:T(128)} %bitcast.1.place_ref, f32[256,1024]{1,0:T(8,128)} %bitcast.25, s32[4,32]{1,0:T(4,128)} %bitcast.26, f32[4,32]{1,0:T(4,128)} %bitcast.27), custom_call_target="tpu_custom_call" | custom-call | tf_op jit(solution)/shard_map/pack/pallas_call | solution.py:271
  1.5 0.0 copy-start.5
  1.5 27.9 %all_to_all.15 = f32[64,17,2,128]{3,2,1,0:T(2,128)S(1)} all-to-all(f32[64,17,2,128]{3,2,1,0:T(2,128)S(1)} %bitcast.17), channel_id=1, replica_groups={{308,278,310,280,312,282,314,284,316,286,318,0,32,2,34,4,36,6,38,8,40,1..., dimensions={0} | all-to-all | bytes 2228224 | tf_op jit(solution)/shard_map/all_to_all | solution.py:291
  29.4 0.0 copy-start
  29.4 0.0 copy-start.1
  29.4 0.0 copy-start.2
  29.5 0.0 copy-start.3
  29.5 0.0 copy-start.4
  29.5 0.9 %stack.1 = f32[264,128]{1,0:T(8,128)S(1)} custom-call(f32[2176,128]{1,0:T(8,128)S(1)} %bitcast.18), custom_call_target="tpu_custom_call" | custom-call | tf_op jit(solution)/shard_map/stack/pallas_call | solution.py:294
  30.4 20.1 %all_to_all.16 = f32[8,33,1,128]{3,2,1,0:T(1,128)S(1)} all-to-all(f32[8,33,1,128]{3,2,1,0:T(1,128)S(1)} %bitcast.20), channel_id=1, replica_groups={{65,64,1,0,129,128,193,192},{67,66,3,2,131,130,195,194},{69,68,5,4,133,..., dimensions={0} | all-to-all | bytes 270336 | tf_op jit(solution)/shard_map/all_to_all | solution.py:302
  50.5 0.6 sum.1
  51.1 9.6 %all-to-all-start.2 = ((f32[64,1,128]{2,1,0:T(1,128)}), f32[64,1,128]{2,1,0:T(1,128)S(1)}, u32[]{:S(2)}, u32[]{:S(2)}) async-start(f32[64,1,128]{2,1,0:T(1,128)} %bitcast.10), calls=%async_computation.2 | async-start | bytes 65536 | tf_op jit(solution)/shard_map/all_to_all | solution.py:316
  60.8 0.0 copy-done.5
  60.8 0.1 reshape.39
  60.9 3.2 %all-to-all-done.2 = f32[64,1,128]{2,1,0:T(1,128)S(1)} async-done(((f32[64,1,128]{2,1,0:T(1,128)}), f32[64,1,128]{2,1,0:T(1,128)S(1)}, u32[]{:S(2)}, u32[]{:S(2)}) %all-to-all-start.2) | async-done | bytes 32800 | tf_op jit(solution)/shard_map/all_to_all | solution.py:316
  64.1 0.0 copy-done
  64.1 0.0 copy-done.1
  64.1 0.0 copy-done.2
  64.1 0.0 copy-done.3
  64.1 0.0 copy-done.4
  64.1 1.6 %image.1 = f32[384,128]{1,0:T(8,128)} custom-call(s32[1]{0:T(128)} %bitcast.tile_ref, f32[64,128]{1,0:T(8,128)S(1)} %bitcast.22, f32[1,128]{1,0:T(1,128)S(1)} %get-tuple-element.8.counts_ref, f32[8,128]{1,0:T(8,128)S(1)} %bitcast.23, f32[8,128]{1,0:T(8,128)S(1)} %copy-done.3, f32[8,128]{1,0:T(8,128)S(1)} %copy-done.4, f32[256,256]{1,0:T(8,128)S(1)} %copy-done.1, ...), custom_call_target="tpu_custom_call" | custom-call | tf_op jit(solution)/shard_map/image/pallas_call | solution.py:319
  (1 shorter events, 0.0 us)
Async XLA Ops:
  1.5 59.3 %copy-start.5 = (f32[1024]{0:T(1024)S(1)}, f32[1024]{0:T(1024)}, u32[]{:S(2)}) copy-start(f32[1024]{0:T(1024)} %param.10) | copy-start | bytes 12292
  29.4 34.7 %copy-start = (f32[1,1024,384]{2,1,0:T(8,128)S(1)}, f32[1,1024,384]{2,1,0:T(8,128)}, u32[]{:S(2)}) copy-start(f32[1,1024,384]{2,1,0:T(8,128)} %param.13) | copy-start | bytes 4718596
  29.4 34.7 %copy-start.1 = (f32[256,256]{1,0:T(8,128)S(1)}, f32[256,256]{1,0:T(8,128)}, u32[]{:S(2)}) copy-start(f32[256,256]{1,0:T(8,128)} %constant.53.clone.table_ref) | copy-start | bytes 786436
  29.4 34.7 %copy-start.2 = (f32[1,8,128]{2,1,0:T(8,128)S(1)}, f32[1,8,128]{2,1,0:T(8,128)}, u32[]{:S(2)}) copy-start(f32[1,8,128]{2,1,0:T(8,128)} %param.14) | copy-start | bytes 12292
  29.5 34.7 %copy-start.3 = (f32[8,128]{1,0:T(8,128)S(1)}, f32[8,128]{1,0:T(8,128)}, u32[]{:S(2)}) copy-start(f32[8,128]{1,0:T(8,128)} %constant.51.clone.turn_cos_ref) | copy-start | bytes 12292
  29.5 34.7 %copy-start.4 = (f32[8,128]{1,0:T(8,128)S(1)}, f32[8,128]{1,0:T(8,128)}, u32[]{:S(2)}) copy-start(f32[8,128]{1,0:T(8,128)} %constant.52.clone.turn_sin_ref) | copy-start | bytes 12292
  51.1 13.0 %all-to-all-start.2 = ((f32[64,1,128]{2,1,0:T(1,128)}), f32[64,1,128]{2,1,0:T(1,128)S(1)}, u32[]{:S(2)}, u32[]{:S(2)}) async-start(f32[64,1,128]{2,1,0:T(1,128)} %bitcast.10), calls=%async_computation.2 | async-start | bytes 65536 | tf_op jit(solution)/shard_map/all_to_all | solution.py:316

commit v8 on v7

--- a/solution.py
+++ b/solution.py
@@ -174,7 +174,9 @@
     table_ref,
     spread_ref,
     weights_ref,
-    out_ref,
+    out_hbm,
+    slab_ref,
+    sems,
 ):
     samples = RADIX * LANES
     parts = [stacked_ref[pl.ds(j, 8, stride=RADIX), :] for j in range(RADIX)]
@@ -240,15 +242,24 @@
     fold = jnp.sum(
         jnp.where(lane == tile_ref[0], counts_ref[0:1, :], 0.0), axis=1, keepdims=True
     )
-    focused = product(*halves(filtered), *halves(weights_ref[...])) / jnp.sqrt(fold)
-    focused_high, focused_low = halves(focused)
+    filtered = halves(filtered)
     spread_high, spread_low = halves(spread_ref[...])
-    out_ref[...] = lax.dot_general(
-        jnp.concatenate([focused_high, focused_high, focused_low], axis=0),
-        jnp.concatenate([spread_high, spread_low, spread_high], axis=0),
-        (((0,), (0,)), ((), ())),
-        preferred_element_type=jnp.float32,
-    )
+    spread = jnp.concatenate([spread_high, spread_low, spread_high], axis=0)
+    copies = []
+    for i, (low, high) in enumerate(((0, 256), (256, out_hbm.shape[0]))):
+        focused = product(*filtered, *halves(weights_ref[:, low:high])) / jnp.sqrt(fold)
+        focused_high, focused_low = halves(focused)
+        slab_ref[low:high, :] = lax.dot_general(
+            jnp.concatenate([focused_high, focused_high, focused_low], axis=0),
+            spread,
+            (((0,), (0,)), ((), ())),
+            preferred_element_type=jnp.float32,
+        )
+        copy = pltpu.make_async_copy(slab_ref.at[low:high], out_hbm.at[low:high], sems.at[i])
+        copy.start()
+        copies.append(copy)
+    for copy in copies:
+        copy.wait()
 
 
 def fourier_parts():
@@ -320,7 +331,11 @@
         image_kernel,
         out_shape=jax.ShapeDtypeStruct((depth, spread.shape[2]), f32),
         in_specs=[SMEM] + [VMEM] * 8,
-        out_specs=VMEM,
+        out_specs=HBM,
+        scratch_shapes=[
+            pltpu.VMEM((depth, spread.shape[2]), f32),
+            pltpu.SemaphoreType.DMA((2,)),
+        ],
         compiler_params=pltpu.CompilerParams(vmem_limit_bytes=16 * MIB),
         name="image",
     )(

time: 66 us -> 66.1 us (level)
  no operation moved by 1% of the time
where the time goes in v8:
time: 66.1 us; the launch traced here: 65.8 us
  blocking collectives  48 us (73%)
  starting transfers between devices  9.64 us (15%)
  Pallas kernels  4.74 us (7%)
  waiting for transfers between devices  3.18 us (5%)
    all_to_all x1, blocking collectives, body(): lax.all_to_all(sent.reshape(64, -1, 2, LANES), NEAR, 0, 0, axis_index_gro...  27.9 us
    all_to_all x1, blocking collectives, body(): lax.all_to_all(sent.reshape(8, 33, 1, LANES), FAR, 0, 0, axis_index_group...  20.1 us
    all_to_all x1, starting transfers between devices, body(): lax.all_to_all(sent.reshape(64, 1, LANES), NEAR, 0, 0, axis_index_groups=...  9.64 us
    all_to_all x1, waiting for transfers between devices, body(): lax.all_to_all(sent.reshape(64, 1, LANES), NEAR, 0, 0, axis_index_groups=...  3.18 us
    pallas_call x1, Pallas kernels, body(): pl.pallas_call(image_kernel, out_shape=jax.ShapeDtypeStruct((depth, sprea...  1.68 us
    pallas_call x1, Pallas kernels, body(): pl.pallas_call(pack_kernel, out_shape=jax.ShapeDtypeStruct((64 * (blocks...  1.49 us
  transfers between devices with their start and end apart: 1, of which 1 were waited for; matrix products, arithmetic and copies ran while one was open for 0% of the time, Pallas kernels for 0%

profile of v8, /device:TPU:1, one launch (start us, length us, event | category | flops | bytes accessed | tf_op | source)
XLA Modules:
  0.0 65.8 jit_solution(23307476405018801)
XLA Ops:
  0.0 1.5 %pack.1 = f32[2176,128]{1,0:T(8,128)S(1)} custom-call(s32[1]{0:T(128)} %bitcast.1.place_ref, f32[256,1024]{1,0:T(8,128)} %bitcast.25, s32[4,32]{1,0:T(4,128)} %bitcast.26, f32[4,32]{1,0:T(4,128)} %bitcast.27), custom_call_target="tpu_custom_call" | custom-call | tf_op jit(solution)/shard_map/pack/pallas_call | solution.py:282
  1.5 0.0 copy-start.5
  1.5 27.9 %all_to_all.15 = f32[64,17,2,128]{3,2,1,0:T(2,128)S(1)} all-to-all(f32[64,17,2,128]{3,2,1,0:T(2,128)S(1)} %bitcast.17), channel_id=1, replica_groups={{308,278,310,280,312,282,314,284,316,286,318,0,32,2,34,4,36,6,38,8,40,1..., dimensions={0} | all-to-all | bytes 2228224 | tf_op jit(solution)/shard_map/all_to_all | solution.py:302
  29.4 0.0 copy-start
  29.4 0.0 copy-start.1
  29.4 0.0 copy-start.2
  29.5 0.0 copy-start.3
  29.5 0.0 copy-start.4
  29.5 0.9 %stack.1 = f32[264,128]{1,0:T(8,128)S(1)} custom-call(f32[2176,128]{1,0:T(8,128)S(1)} %bitcast.18), custom_call_target="tpu_custom_call" | custom-call | tf_op jit(solution)/shard_map/stack/pallas_call | solution.py:305
  30.4 20.1 %all_to_all.16 = f32[8,33,1,128]{3,2,1,0:T(1,128)S(1)} all-to-all(f32[8,33,1,128]{3,2,1,0:T(1,128)S(1)} %bitcast.20), channel_id=1, replica_groups={{65,64,1,0,129,128,193,192},{67,66,3,2,131,130,195,194},{69,68,5,4,133,..., dimensions={0} | all-to-all | bytes 270336 | tf_op jit(solution)/shard_map/all_to_all | solution.py:313
  50.5 0.6 sum.1
  51.1 9.6 %all-to-all-start.2 = ((f32[64,1,128]{2,1,0:T(1,128)}), f32[64,1,128]{2,1,0:T(1,128)S(1)}, u32[]{:S(2)}, u32[]{:S(2)}) async-start(f32[64,1,128]{2,1,0:T(1,128)} %bitcast.10), calls=%async_computation.2 | async-start | bytes 65536 | tf_op jit(solution)/shard_map/all_to_all | solution.py:327
  60.8 0.0 copy-done.5
  60.8 0.1 reshape.39
  60.9 3.2 %all-to-all-done.2 = f32[64,1,128]{2,1,0:T(1,128)S(1)} async-done(((f32[64,1,128]{2,1,0:T(1,128)}), f32[64,1,128]{2,1,0:T(1,128)S(1)}, u32[]{:S(2)}, u32[]{:S(2)}) %all-to-all-start.2) | async-done | bytes 32800 | tf_op jit(solution)/shard_map/all_to_all | solution.py:327
  64.1 0.0 copy-done
  64.1 0.0 copy-done.1
  64.1 0.0 copy-done.2
  64.1 0.0 copy-done.3
  64.1 0.0 copy-done.4
  64.1 1.7 %image.1 = f32[384,128]{1,0:T(8,128)} custom-call(s32[1]{0:T(128)} %bitcast.tile_ref, f32[64,128]{1,0:T(8,128)S(1)} %bitcast.22, f32[1,128]{1,0:T(1,128)S(1)} %get-tuple-element.8.counts_ref, f32[8,128]{1,0:T(8,128)S(1)} %bitcast.23, f32[8,128]{1,0:T(8,128)S(1)} %copy-done.3, f32[8,128]{1,0:T(8,128)S(1)} %copy-done.4, f32[256,256]{1,0:T(8,128)S(1)} %copy-done.1, ...), custom_call_target="tpu_custom_call" | custom-call | tf_op jit(solution)/shard_map/image/pallas_call | solution.py:330
  (1 shorter events, 0.0 us)
Async XLA Ops:
  1.5 59.3 %copy-start.5 = (f32[1024]{0:T(1024)S(1)}, f32[1024]{0:T(1024)}, u32[]{:S(2)}) copy-start(f32[1024]{0:T(1024)} %param.10) | copy-start | bytes 12292
  29.4 34.7 %copy-start = (f32[1,1024,384]{2,1,0:T(8,128)S(1)}, f32[1,1024,384]{2,1,0:T(8,128)}, u32[]{:S(2)}) copy-start(f32[1,1024,384]{2,1,0:T(8,128)} %param.13) | copy-start | bytes 4718596
  29.4 34.7 %copy-start.1 = (f32[256,256]{1,0:T(8,128)S(1)}, f32[256,256]{1,0:T(8,128)}, u32[]{:S(2)}) copy-start(f32[256,256]{1,0:T(8,128)} %constant.53.clone.table_ref) | copy-start | bytes 786436
  29.4 34.7 %copy-start.2 = (f32[1,8,128]{2,1,0:T(8,128)S(1)}, f32[1,8,128]{2,1,0:T(8,128)}, u32[]{:S(2)}) copy-start(f32[1,8,128]{2,1,0:T(8,128)} %param.14) | copy-start | bytes 12292
  29.5 34.7 %copy-start.3 = (f32[8,128]{1,0:T(8,128)S(1)}, f32[8,128]{1,0:T(8,128)}, u32[]{:S(2)}) copy-start(f32[8,128]{1,0:T(8,128)} %constant.51.clone.turn_cos_ref) | copy-start | bytes 12292
  29.5 34.7 %copy-start.4 = (f32[8,128]{1,0:T(8,128)S(1)}, f32[8,128]{1,0:T(8,128)}, u32[]{:S(2)}) copy-start(f32[8,128]{1,0:T(8,128)} %constant.52.clone.turn_sin_ref) | copy-start | bytes 12292
  51.1 13.0 %all-to-all-start.2 = ((f32[64,1,128]{2,1,0:T(1,128)}), f32[64,1,128]{2,1,0:T(1,128)S(1)}, u32[]{:S(2)}, u32[]{:S(2)}) async-start(f32[64,1,128]{2,1,0:T(1,128)} %bitcast.10), calls=%async_computation.2 | async-start | bytes 65536 | tf_op jit(solution)/shard_map/all_to_all | solution.py:327
